TPU v7x, 32 devices: a whole 2x2x4 slice. The times are simulated.
32 devices in a mesh: seq: 4 (over x, core), head: 8 (over z, y).
Axes of the slice: x: 2, y: 2, z: 4, core: 2. Of those that a mesh axis runs over, the one named last changes fastest.
Arguments:
- qk_in: bfloat16 [4, 4096, 2, 2048], P(None, 'seq', None, 'head'), may hold values from -6 to 6
- v_in: bfloat16 [4, 4096, 4096], P(None, 'seq', 'head'), may hold values from -6 to 6
- gate_z: bfloat16 [4, 4096, 4096], P(None, 'seq', 'head'), may hold values from -6 to 6
- conv_qk: bfloat16 [4, 2, 2048], P(None, None, 'head'), may hold values from -3 to 3
- conv_v: bfloat16 [4, 4096], P(None, 'head'), may hold values from -3 to 3
- log_decay: float32 [4, 32, 4096], P(None, 'head', 'seq'), may hold values from -0.7 to 0
- write_gain: float32 [4, 32, 4096], P(None, 'head', 'seq'), may hold values from 0 to 1
- norm_gain: float32 [128], replicated, may hold values from 0.5 to 1.5
- prompt_lengths: int32 [4], replicated, may hold values from 1 to 4096, 10240 in all
- placement: int32 [4, 8], P('seq'), may hold values from 0 to 3
Outputs:
- attended: bfloat16 [4, 4096, 4096], P(None, 'seq', 'head')
- rollout_state: float32 [4, 8, 32, 128, 128], P('seq', 'head')
Inputs may be any that keep to these rules, and one draw needn't show every extreme that they name: `prompt_lengths`: the largest length is exactly 4096; the lengths sum to 10240. Device (s, r) serves prompt placement[s, r]; the values 0 and 3 each occur at least once.
All inputs are finite; a program needn't handle non-finite values.
Results may differ from a plain program's by a relative error of at most 0.02.
Values may be sent and summed in bfloat16 or wider, within the bound.
No kernel may reach another device: no remote copies, remote signals or barrier semaphores. Data moves between devices by JAX's collectives and lax.ppermute only.
A program may use at most 128 MiB of HBM per device.

v0:
```python
import functools

import jax
import jax.numpy as jnp
from jax import lax
from jax.experimental import pallas as pl
from jax.experimental.pallas import tpu as pltpu
from jax.sharding import PartitionSpec as P

DK = 128
DV = 128
CONV = 4
BLOCK = 128
TINY = 16
EDGE = 8
EPSILON = 1e-06
VMEM_BYTES = 40 * 1024 * 1024
SMALL_VMEM_BYTES = 8 * 1024 * 1024
F32 = jnp.float32
BF16 = jnp.bfloat16


def far(x):
    return pltpu.with_memory_space_constraint(x, pltpu.HBM)


def dot(a, b):
    return lax.dot_general(a, b, (((1,), (0,)), ((), ())), preferred_element_type=F32)


def silu(x):
    half = 0.5 * x
    return half + half * jnp.tanh(half)


def mixed_rows(pad_ref, taps, rim, first, step, c):
    total = None
    for i in range(CONV):
        start = rim + first + step * (c * BLOCK + i - (CONV - 1))
        stride = None if step == 1 else step
        term = pad_ref[pl.ds(start, BLOCK, stride), :] * taps[i]
        total = term if total is None else total + term
    return silu(total)


def unit_rows(x):
    return x * lax.rsqrt(jnp.sum(x * x, axis=-1, keepdims=True) + EPSILON)


def heads_rows(ref, head, group):
    every = ref[0]
    rows = every[:group]
    for n in range(1, every.shape[0] // group):
        rows = jnp.where(head == n, every[n * group : (n + 1) * group], rows)
    return rows


def gates_of_heads(log_ref, gain_ref, used, head, group):
    log = heads_rows(log_ref, head, group)
    lane = lax.broadcasted_iota(jnp.int32, log.shape, 1)
    valid = lane < used
    cum = jnp.where(valid, log, 0.0)
    gain = jnp.where(valid, heads_rows(gain_ref, head, group), 0.0)
    shift = 1
    while shift < BLOCK:
        cum = cum + jnp.where(lane % BLOCK >= shift, pltpu.roll(cum, shift, 1), 0.0)
        shift *= 2
    return cum, gain


def as_columns(rows, chunks):
    parts = [rows[:, c * BLOCK : (c + 1) * BLOCK] for c in range(chunks)]
    short = BLOCK - 8 * chunks
    if short:
        parts.append(jnp.zeros((short, BLOCK), F32))
    return jnp.concatenate(parts, axis=0).T


def block_bases(parts, chunks):
    rows = jnp.concatenate(parts, axis=0)
    short = 7 - rows.shape[0]
    fill = [jnp.zeros((short, rows.shape[1]), F32)] if short else []
    rows = jnp.concatenate([rows] + fill + [jnp.ones((1, rows.shape[1]), F32)], axis=0)
    return [rows[:, c * BLOCK : (c + 1) * BLOCK] for c in range(chunks)]


def spread_squares(base, group, kinds):
    high = base.astype(BF16).astype(F32)
    middle = (base - high).astype(BF16).astype(F32)
    low = base - high - middle
    parts = [high, middle, low]
    row = lax.broadcasted_iota(jnp.int32, (32, BLOCK), 0)
    which = row % 8
    real = row < 24
    stacked = jnp.concatenate(parts + [jnp.zeros_like(high)], axis=0)
    left = jnp.where(jnp.logical_and(which == 7, real), 1.0, stacked).T.astype(BF16)
    blocks = []
    for h in range(group):
        minus = jnp.concatenate([jnp.broadcast_to(-part[h : h + 1], (8, BLOCK)) for part in parts + [low]], axis=0)
        blocks.append(jnp.where(which == h, 1.0, jnp.where(which == 7, minus, 0.0)))
    for n in range(group, group * kinds):
        blocks.append(jnp.where(which == n, 1.0, 0.0).astype(F32))
    every = dot(left, jnp.concatenate(blocks, axis=1).astype(BF16))
    return [every[:, n * BLOCK : (n + 1) * BLOCK] for n in range(group * kinds)]


def mix(qk_ref, halo_ref, taps_ref, qn_ref, kn_ref, raw_scr, key_heads, chunks):
    kinds = 2 * key_heads
    rim = 2 * EDGE
    taps = taps_ref[...].astype(F32)
    raw_scr[:rim] = halo_ref[0].astype(F32)[:rim]
    raw_scr[rim:] = qk_ref[0].astype(F32)
    for c in range(chunks):
        span = slice(c * BLOCK, (c + 1) * BLOCK)
        for kind in range(kinds):
            own = [taps[n : n + 1] for n in range(kind, taps.shape[0], kinds)]
            rows = unit_rows(mixed_rows(raw_scr, own, rim, kind, kinds, c))
            to_ref = kn_ref if kind % 2 else qn_ref
            to_ref[0, span, kind // 2 * DK : (kind // 2 + 1) * DK] = rows.astype(BF16)


def weave(*lists):
    places = []
    for which, entries in enumerate(lists):
        places += [((n + 0.5) / len(entries), which, n) for n in range(len(entries))]
    for _, which, n in sorted(places):
        lists[which][n]()


def prepare_kernel(first, count, head, group, chunks, key_heads, mixes, *refs):
    length_ref, v_ref, halo_ref, v_taps_ref, log_ref, gain_ref, after_ref = refs[:7]
    refs = refs[7:]
    if mixes:
        qk_ref, qk_taps_ref, wu_ref, start_ref, map_ref, qn_ref, kn_ref = refs[:7]
        v_pad, m_scr, b_scr, fade_scr, st_scr, a_scr, x_scr, y_scr, raw_scr = refs[7:]
        key_columns = slice(head * DK, (head + 1) * DK)
    else:
        kn_ref, wu_ref, start_ref, map_ref = refs[:4]
        v_pad, m_scr, b_scr, fade_scr, st_scr, a_scr, x_scr, y_scr = refs[4:]
        key_columns = slice(0, DK)
    step = pl.program_id(0)
    used = length_ref[first + jnp.minimum(step, count - 1)] - lax.axis_index("seq") * (chunks * BLOCK)
    units = [(h, c) for c in range(chunks) for h in range(group)]
    slot = step % 2
    live = jnp.logical_and(step < count, used > 0)

    def begin():
        row = lax.broadcasted_iota(jnp.int32, (DV + DK, DK), 0)
        lane = lax.broadcasted_iota(jnp.int32, (DV + DK, DK), 1)
        for h in range(group):
            st_scr[h] = jnp.where(row == lane + DV, 1.0, 0.0).astype(F32)

    def advance(c):
        narrow, moved = {}, {}

        def load(h):
            narrow[h] = st_scr[h].astype(BF16)
            start_ref[0, h, c * (DV + DK) : (c + 1) * (DV + DK), :] = narrow[h]

        def move(h):
            moved[h] = dot(narrow[h], m_scr[1 - slot, c, h])

        def store(h):
            fade = fade_scr[1 - slot, c, h : h + 1, :]
            state = st_scr[h, :DV] * fade + (moved[h][:DV] + b_scr[1 - slot, c, h])
            trans = st_scr[h, DV:] * fade + moved[h][DV:]
            if c < chunks - 1:
                st_scr[h, :DV] = state
                st_scr[h, DV:] = trans
            else:
                map_ref[h, :DV] = state.astype(BF16)
                map_ref[h, DV:] = trans.astype(BF16)

        return [functools.partial(act, h) for act in (load, move, store) for h in range(group)]

    recurrence = [begin]
    for c in range(chunks):
        recurrence += advance(c)

    @pl.when(jnp.logical_not(live))
    def _():
        @pl.when(step > 0)
        def _():
            weave(recurrence)

        @pl.when(step < count)
        def _():
            if mixes:
                qn_ref[...] = jnp.zeros_like(qn_ref)
                kn_ref[...] = jnp.zeros_like(kn_ref)
            wu_ref[...] = jnp.zeros_like(wu_ref)
            fade_scr[slot] = jnp.ones(fade_scr.shape[1:], F32)
            m_scr[slot] = jnp.zeros(m_scr.shape[1:], BF16)
            b_scr[slot] = jnp.zeros(b_scr.shape[1:], F32)

    @pl.when(live)
    def _():
        if mixes:
            mix(qk_ref, halo_ref, qk_taps_ref, qn_ref, kn_ref, raw_scr, key_heads, chunks)
        halo = halo_ref[0].astype(F32)
        v_pad[EDGE:, :] = v_ref[0].astype(F32)
        for i in range(CONV - 1):
            for h in range(group):
                source = 2 * EDGE + (i * key_heads + head) * group + h
                v_pad[EDGE - CONV + 1 + i : EDGE - CONV + 2 + i, h * DV : (h + 1) * DV] = halo[
                    source : source + 1
                ]
        v_all_taps = v_taps_ref[...].astype(F32)
        v_taps = [v_all_taps[i : i + 1] for i in range(CONV)]

        cum, gain = gates_of_heads(log_ref, gain_ref, used, head, group)
        both_gains = gain * jnp.exp(cum)
        columns = as_columns(jnp.concatenate([cum] * (8 // group), axis=0), chunks)

        def span(c):
            return slice(c * BLOCK, (c + 1) * BLOCK)

        row = lax.broadcasted_iota(jnp.int32, (BLOCK, BLOCK), 0)
        lane = lax.broadcasted_iota(jnp.int32, (BLOCK, BLOCK), 1)
        above = row < lane
        small_row = lax.broadcasted_iota(jnp.int32, (TINY, BLOCK), 0)
        small_lane = lax.broadcasted_iota(jnp.int32, (TINY, BLOCK), 1)
        part_of = small_lane // TINY
        tiny_eye = jnp.where(small_row == small_lane % TINY, 1.0, 0.0).astype(F32)

        keys = [kn_ref[0, span(c), key_columns] for c in range(chunks)]
        turned = {}

        def front(some):
            ops, kk, compact, solved, mixed = [], {}, {}, {}, {}
            local = [(h, c) for c in some for h in range(group)]

            def start(c):
                turned[c] = keys[c].T
                kk[c] = dot(keys[c], turned[c])

            def mask(h, c):
                r = h * chunks + c
                ratio = jnp.exp(cum[h : h + 1, span(c)] - columns[:, c * 8 + h : c * 8 + h + 1])
                strict = jnp.where(above, ratio * kk[c] * -gain[h : h + 1, span(c)], 0.0)
                a_scr[r] = strict.astype(BF16)
                tiny = strict[0:TINY]
                for b in range(1, BLOCK // TINY):
                    tiny = jnp.where(part_of == b, strict[b * TINY : (b + 1) * TINY], tiny)
                compact[r] = tiny
                solved[r] = tiny_eye

            def eliminate(j, r):
                factor = jnp.take_along_axis(compact[r], part_of * TINY + j, axis=1, mode="promise_in_bounds")
                solved[r] = solved[r] + factor * solved[r][j : j + 1, :]

            def place(r):
                for b in range(BLOCK // TINY):
                    x_scr[r, b * TINY : (b + 1) * TINY, :] = jnp.where(part_of == b, solved[r], 0.0).astype(BF16)

            def convolve(c):
                mixed[c] = mixed_rows(v_pad, v_taps, EDGE, 0, 1, c).astype(BF16)

            def scale(h, c):
                top = h * (DK + DV)
                v_wide = mixed[c][:, h * DV : (h + 1) * DV].T.astype(F32)
                y_scr[c, top : top + DK, :] = (turned[c].astype(F32) * both_gains[h : h + 1, span(c)]).astype(BF16)
                y_scr[c, top + DK : top + DK + DV, :] = (v_wide * gain[h : h + 1, span(c)]).astype(BF16)

            for c in some:
                ops.append(functools.partial(start, c))
            for h, c in local:
                ops.append(functools.partial(mask, h, c))
            for j in range(TINY - 1, 0, -1):
                for h, c in local:
                    ops.append(functools.partial(eliminate, j, h * chunks + c))
            for h, c in local:
                ops.append(functools.partial(place, h * chunks + c))
            right = []
            for c in some:
                right.append(functools.partial(convolve, c))
                right += [functools.partial(scale, h, c) for h in range(group)]
            return ops, right

        def back(some):
            ops, own, moved = [], {}, {}
            local = [(h, c) for c in some for h in range(group)]

            def reach(size, r):
                half_lane = lax.broadcasted_iota(jnp.int32, (BLOCK // 2, BLOCK), 1)
                half_row = lax.broadcasted_iota(jnp.int32, (BLOCK // 2, BLOCK), 0)
                partner = half_lane // size == 2 * (half_row // size) + 1
                own[r] = jnp.concatenate([x_scr[r, s : s + size, :] for s in range(0, BLOCK, 2 * size)], axis=0)
                moved[r] = jnp.where(partner, dot(own[r], a_scr[r]), 0.0).astype(BF16)

            def join(size, r):
                update = own[r] + dot(moved[r], x_scr[r]).astype(BF16)
                for n, s in enumerate(range(0, BLOCK, 2 * size)):
                    x_scr[r, s : s + size, :] = update[n * size : (n + 1) * size]

            def solve(h, c):
                r = h * chunks + c
                top = h * (DK + DV)
                sums = cum[:, span(c)]
                last = sums[:, BLOCK - 1 : BLOCK]
                tail = jnp.exp(last - sums)
                fade = jnp.broadcast_to(jnp.exp(last), (group, BLOCK))
                rows = dot(y_scr[c, top : top + DK + DV, :], x_scr[r])
                wu_ref[0, r] = rows.astype(BF16)
                y_scr[c, top : top + DK + DV, :] = (rows * tail[h : h + 1]).astype(BF16)
                fade_scr[slot, c, h : h + 1, :] = fade[h : h + 1]

            def finish(c):
                both = dot(y_scr[c], keys[c])
                for h in range(group):
                    top = h * (DK + DV)
                    m_scr[slot, c, h] = (-both[top : top + DK]).astype(BF16)
                    b_scr[slot, c, h] = both[top + DK : top + DK + DV]

            size = TINY
            while size < BLOCK:
                ops += [functools.partial(reach, size, h * chunks + c) for h, c in local]
                ops += [functools.partial(join, size, h * chunks + c) for h, c in local]
                size *= 2
            ops += [functools.partial(solve, h, c) for h, c in local]
            ops += [functools.partial(finish, c) for c in some]
            return ops

        half = chunks // 2
        early, late = range(half), range(half, chunks)
        early_front, early_right = front(early)
        late_front, late_right = front(late)
        cut = len(recurrence) // 3
        weave(early_front, recurrence[:cut], early_right)
        weave(back(early), late_front, late_right)
        weave(back(late), recurrence[cut:])


def prepare(job, lengths, qk_rows, v_in, halo, qk_taps, v_taps, log_decay, write_gain, key_heads, mixed, after):
    head, first, count = job
    tok = v_in.shape[1]
    value_heads = v_in.shape[2] // DV
    group = value_heads // key_heads
    chunks = tok // BLOCK
    rows = group * chunks
    wide = group * DV
    mixes = mixed is None

    def now(i):
        return jnp.minimum(i, count - 1)

    def before(i):
        return jnp.maximum(i - 1, 0)

    def whole_of(i, lengths):
        return (first + now(i), 0, 0)

    operands = [far(v_in), halo, far(v_taps), far(log_decay), far(write_gain), far(after)]
    in_specs = [
        pl.BlockSpec((1, tok, wide), lambda i, lengths: (first + now(i), 0, head)),
        pl.BlockSpec((1,) + halo.shape[1:], whole_of),
        pl.BlockSpec((CONV, wide), lambda i, lengths: (0, head)),
        pl.BlockSpec((1, value_heads, tok), whole_of),
        pl.BlockSpec((1, value_heads, tok), whole_of),
        pl.BlockSpec(memory_space=pltpu.HBM),
    ]
    out_specs = [
        pl.BlockSpec((1, rows, DK + DV, BLOCK), lambda i, lengths: (now(i), 0, 0, 0)),
        pl.BlockSpec((1, group, chunks * (DV + DK), DK), lambda i, lengths: (before(i), 0, 0, 0)),
        pl.BlockSpec((group, DV + DK, DK), lambda i, lengths: (before(i), 0, 0)),
    ]
    out_shape = [
        pltpu.HBM((count, rows, DK + DV, BLOCK), BF16),
        pltpu.HBM((count, group, chunks * (DV + DK), DK), BF16),
        jax.ShapeDtypeStruct((count * group, DV + DK, DK), BF16),
    ]
    scratch = [
        pltpu.VMEM((tok + EDGE, wide), F32),
        pltpu.VMEM((2, chunks, group, DK, DK), BF16),
        pltpu.VMEM((2, chunks, group, DV, DK), F32),
        pltpu.VMEM((2, chunks, group, BLOCK), F32),
        pltpu.VMEM((group, DV + DK, DK), F32),
        pltpu.VMEM((rows, BLOCK, BLOCK), BF16),
        pltpu.VMEM((rows, BLOCK, BLOCK), BF16),
        pltpu.VMEM((chunks, group * (DK + DV), BLOCK), BF16),
    ]
    if mixes:
        operands += [far(qk_rows), far(qk_taps)]
        in_specs += [
            pl.BlockSpec((1,) + qk_rows.shape[1:], whole_of),
            pl.BlockSpec(qk_taps.shape, lambda i, lengths: (0, 0)),
        ]
        out_specs += [pl.BlockSpec((1, tok, key_heads * DK), lambda i, lengths: (now(i), 0, 0))] * 2
        out_shape += [pltpu.HBM((count, tok, key_heads * DK), BF16)] * 2
        scratch.append(pltpu.VMEM((qk_rows.shape[1] + 2 * EDGE, DK), F32))
    else:
        operands.append(far(mixed))
        in_specs.append(pl.BlockSpec((1, tok, DK), lambda i, lengths: (first + now(i), 0, head)))
    return pl.pallas_call(
        functools.partial(prepare_kernel, first, count, head, group, chunks, key_heads, mixes),
        grid_spec=pltpu.PrefetchScalarGridSpec(
            num_scalar_prefetch=1,
            grid=(count + 1,),
            in_specs=in_specs,
            out_specs=out_specs,
            scratch_shapes=scratch,
        ),
        out_shape=out_shape,
        compiler_params=pltpu.CompilerParams(vmem_limit_bytes=VMEM_BYTES),
        cost_estimate=pl.CostEstimate(flops=5 * 10**9 * count, bytes_accessed=4 * 2**20 * count, transcendentals=10**6),
        name="prepare",
    )(lengths, *operands)


def outputs_kernel(
    first, head, group, chunks,
    length_ref, qn_ref, kn_ref, wu_ref, start_ref, log_ref, gain_ref, enter_ref, z_ref, norm_ref, held_ref, after_ref,
    out_ref,
    first_scr, score_scr, seen_scr,
):
    used = length_ref[first + pl.program_id(0)] - lax.axis_index("seq") * (chunks * BLOCK)
    units = [(h, c) for c in range(chunks) for h in range(group)]

    @pl.when(used <= 0)
    def _():
        out_ref[...] = jnp.zeros_like(out_ref)

    @pl.when(used > 0)
    def _():
        cum, gain = gates_of_heads(log_ref, gain_ref, used, head, group)
        faded = jnp.exp(cum)
        columns = as_columns(jnp.concatenate([cum] * (8 // group), axis=0), chunks)
        row = lax.broadcasted_iota(jnp.int32, (BLOCK, BLOCK), 0)
        lane = lax.broadcasted_iota(jnp.int32, (BLOCK, BLOCK), 1)
        upto = row <= lane
        norm_gain = norm_ref[...]

        def span(c):
            return slice(c * BLOCK, (c + 1) * BLOCK)

        for c in range(chunks):
            turned = qn_ref[0, span(c), :].T
            kq = dot(kn_ref[0, span(c), :], turned)
            q_wide = turned.astype(F32)
            for h in range(group):
                r = h * chunks + c
                ratio = jnp.exp(cum[h : h + 1, span(c)] - columns[:, c * 8 + h : c * 8 + h + 1])
                score_scr[r] = jnp.where(upto, ratio * kq, 0.0).astype(BF16)
                seen_scr[r] = q_wide * faded[h : h + 1, span(c)]
                top = c * (DV + DK)
                moved = dot(enter_ref[h], start_ref[0, h, top + DV : top + DV + DK, :])
                first_scr[r] = (moved + start_ref[0, h, top : top + DV, :].astype(F32)).astype(BF16)
        both, raws = {}, {}
        for h, c in units:
            r = h * chunks + c
            both[r] = dot(wu_ref[0, r], score_scr[r])
        for h, c in units:
            r = h * chunks + c
            seen = (seen_scr[r] - both[r][:DK]).astype(BF16)
            raw = dot(first_scr[r], seen) + both[r][DK:]
            mean = jnp.sum(raw * raw, axis=0, keepdims=True) * (1.0 / DV)
            raws[r] = (raw * lax.rsqrt(mean + EPSILON)).astype(BF16)
        for h, c in units:
            scaled = raws[h * chunks + c].T.astype(F32)
            cols = slice(h * DV, (h + 1) * DV)
            gated = scaled * norm_gain * silu(z_ref[0, span(c), cols].astype(F32))
            out_ref[0, span(c), cols] = jnp.where(row + c * BLOCK < used, gated, 0.0).astype(BF16)


def outputs(
    job, piece, lengths, qn, kn, wu, starts, log_decay, write_gain, enter, gate_z, norm_gain, key_heads, held, after,
):
    head, first, _ = job
    begin, count = piece
    prompts, tok, width = gate_z.shape
    rows = wu.shape[1]
    chunks = tok // BLOCK
    group = rows // chunks
    wide = group * DV
    value_heads = key_heads * group
    shift = begin - first
    from_mix = begin if qn.shape[0] == prompts else shift

    def whole_of(i, lengths):
        return (begin + i, 0, 0)

    def wide_of(i, lengths):
        return (begin + i, 0, head)

    def mixed_of(i, lengths):
        return (from_mix + i, 0, head)

    empty = held is None
    return pl.pallas_call(
        functools.partial(outputs_kernel, begin, head, group, chunks),
        grid_spec=pltpu.PrefetchScalarGridSpec(
            num_scalar_prefetch=1,
            grid=(count,),
            in_specs=[
                pl.BlockSpec((1, tok, DK), mixed_of),
                pl.BlockSpec((1, tok, DK), mixed_of),
                pl.BlockSpec((1, rows, DK + DV, BLOCK), lambda i, lengths: (shift + i, 0, 0, 0)),
                pl.BlockSpec((1, group, chunks * (DV + DK), DK), lambda i, lengths: (shift + i, 0, 0, 0)),
                pl.BlockSpec((1, value_heads, tok), whole_of),
                pl.BlockSpec((1, value_heads, tok), whole_of),
                pl.BlockSpec((group, DK, DV), lambda i, lengths: (shift + i, 0, 0)),
                pl.BlockSpec((1, tok, wide), wide_of),
                pl.BlockSpec((1, DV), lambda i, lengths: (0, 0)),
                pl.BlockSpec(memory_space=pltpu.HBM),
                pl.BlockSpec(memory_space=pltpu.HBM),
            ],
            out_specs=pl.BlockSpec((1, tok, wide), wide_of),
            scratch_shapes=[
                pltpu.VMEM((rows, DV, DK), BF16),
                pltpu.VMEM((rows, BLOCK, BLOCK), BF16),
                pltpu.VMEM((rows, BLOCK, DV), F32),
            ],
        ),
        out_shape=pltpu.HBM((prompts, tok, width), BF16),
        input_output_aliases={} if empty else {10: 0},
        compiler_params=pltpu.CompilerParams(vmem_limit_bytes=VMEM_BYTES),
        cost_estimate=pl.CostEstimate(flops=3 * 10**9 * count, bytes_accessed=4 * 2**20 * count, transcendentals=10**6),
        name="outputs",
    )(
        lengths, far(qn), far(kn), far(wu), far(starts), far(log_decay), far(write_gain), enter, far(gate_z),
        far(norm_gain.reshape(1, DV)), far(after if empty else held), far(wu if after is held else after),
    )


def own_chip():
    seq = lax.axis_index("seq")
    return seq // 2, seq % 2 == 1


def early_late(own, other, odd):
    return jnp.where(odd, other, own), jnp.where(odd, own, other)


def follow(there, running):
    return dot(running, there[DV:])


def compose_maps(ins, outs):
    own_ref, other_ref = ins
    _, odd = own_chip()
    for n in range(own_ref.shape[0]):
        early, late = early_late(own_ref[n], other_ref[n], odd)
        both = follow(late, early)
        outs[0][n, :DV] = (both[:DV] + late[:DV].astype(F32)).astype(BF16)
        outs[0][n, DV:] = both[DV:].astype(BF16)


def close_maps(ins, outs):
    own_ref, other_ref = ins[:2]
    refs = ins[2:]
    chips = len(refs)
    chip, odd = own_chip()

    def of_chip(j, n):
        value = refs[0][n]
        for k in range(1, chips):
            value = jnp.where((chip + chips - k) % chips == j, refs[k][n], value)
        return value

    every = range(own_ref.shape[0])
    running = [of_chip(0, n)[:DV] for n in every]
    entering = [jnp.zeros_like(running[n]) for n in every]
    for j in range(1, chips):
        entering = [jnp.where(chip == j, running[n], entering[n]) for n in every]
        there = [of_chip(j, n) for n in every]
        running = [(follow(there[n], running[n]) + there[n][:DV].astype(F32)).astype(BF16) for n in every]
    for n in every:
        early, _ = early_late(own_ref[n], other_ref[n], odd)
        second = (follow(early, entering[n]) + early[:DV].astype(F32)).astype(BF16)
        outs[0][n] = jnp.where(odd, second, entering[n])
        outs[1][n] = running[n].T


def chain_maps(ins, outs):
    count = len(ins)
    mine = lax.axis_index("seq")
    every = range(ins[0].shape[0])

    def run(at):
        running = [ins[at][n, :DV] for n in every]
        for n in every:
            if at == 0:
                outs[0][n] = jnp.zeros_like(running[n])
        for j in range(1, count):
            there = ins[at ^ j]
            if j == at:
                for n in every:
                    outs[0][n] = running[n]
            moved = [follow(there.at[n], running[n]) for n in every]
            running = [(moved[n] + there[n, :DV].astype(F32)).astype(BF16) for n in every]
        for n in every:
            outs[1][n] = running[n].T

    for at in range(count):
        pl.when(mine == at)(functools.partial(run, at))


def choose_finals(group, placement_ref, finals, outs):
    refs = [(ref, n) for ref in finals for n in range(ref.shape[0] // group)]
    for r in range(placement_ref.shape[1]):
        prompt = placement_ref[0, r]
        for p, (ref, n) in enumerate(refs):
            @pl.when(prompt == p)
            def _(ref=ref, n=n):
                outs[0][r] = ref[n * group : (n + 1) * group]


def state_step(placement, group, compose, chain, close, earlier, after):
    operands, shapes = [placement], []
    steps = []
    if compose is not None:
        steps.append(("compose", len(operands), len(compose), len(shapes)))
        operands += compose
        shapes += [compose[0]]
    if chain is not None or close is not None:
        steps.append(("chain" if close is None else "close", len(operands), len(close or chain), len(shapes)))
        close = close or chain
        operands += close
        shapes += [jax.ShapeDtypeStruct((close[0].shape[0], DK, DV), BF16)] * 2
        if earlier is not None:
            steps.append(("choose", len(operands), len(earlier), len(shapes)))
            operands += earlier
            shapes.append(jax.ShapeDtypeStruct((placement.shape[1], group, DK, DV), BF16))
    out_shape = [jax.ShapeDtypeStruct(x.shape, x.dtype) for x in shapes] + [pltpu.HBM((8, 128), F32)]

    def kernel(*refs):
        refs[-1][...] = jnp.zeros_like(refs[-1])
        ins, outs = refs[: len(operands)], refs[len(operands) + 1 :]
        closed = None
        for kind, at, size, to in steps:
            part = ins[at : at + size]
            if kind == "compose":
                compose_maps(part, outs[to : to + 1])
            elif kind in ("close", "chain"):
                (close_maps if kind == "close" else chain_maps)(part, outs[to : to + 2])
                closed = outs[to + 1]
            else:
                choose_finals(group, ins[0], list(part) + [closed], outs[to:])

    vmem = pl.BlockSpec(memory_space=pltpu.VMEM)
    return pl.pallas_call(
        kernel,
        in_specs=[pl.BlockSpec(memory_space=pltpu.SMEM)]
        + [vmem] * (len(operands) - 1)
        + [pl.BlockSpec(memory_space=pltpu.HBM)],
        out_specs=[vmem] * len(out_shape),
        out_shape=out_shape,
        compiler_params=pltpu.CompilerParams(vmem_limit_bytes=SMALL_VMEM_BYTES),
        cost_estimate=pl.CostEstimate(flops=10**9, bytes_accessed=2**20, transcendentals=0),
        name="state_step",
    )(*operands, far(after))


def deliver(parts):
    count, group = parts[0].shape[:2]

    def kernel(*refs):
        for n, ref in enumerate(refs[:-1]):
            refs[-1][:, n * group : (n + 1) * group] = ref[...].astype(F32)

    return pl.pallas_call(
        kernel,
        grid=(2,),
        in_specs=[pl.BlockSpec((count // 2, group, DK, DV), lambda i: (i, 0, 0, 0))] * len(parts),
        out_specs=pl.BlockSpec((count // 2, group * len(parts), DK, DV), lambda i: (i, 0, 0, 0)),
        out_shape=jax.ShapeDtypeStruct((count, group * len(parts), DK, DV), F32),
        compiler_params=pltpu.CompilerParams(vmem_limit_bytes=VMEM_BYTES),
        name="deliver",
    )(*parts)


def across(block, distance):
    count = lax.axis_size("seq")
    return lax.ppermute(block, "seq", [(i, i ^ distance) for i in range(count)])


def from_chip_behind(block, distance):
    count = lax.axis_size("seq")
    chips = count // 2
    route = [(i, ((i // 2 + distance) % chips) * 2 + i % 2) for i in range(count)]
    return lax.ppermute(block, "seq", route)


def shards(
    qk_in, v_in, gate_z, conv_qk, conv_v, log_decay, write_gain, norm_gain, prompt_lengths, placement,
):
    prompts, tok = qk_in.shape[:2]
    key_heads = qk_in.shape[3] // DK
    value_heads = v_in.shape[2] // DV
    rim = CONV - 1
    seq_count = lax.axis_size("seq")
    head_count = lax.axis_size("head")

    def by_head(x):
        x = x.reshape(x.shape[0], x.shape[1], 2, key_heads, DK)
        return jnp.transpose(x, (0, 1, 3, 2, 4)).reshape(x.shape[0], -1, DK)

    qk_rows = by_head(qk_in)
    qk_taps = by_head(conv_qk[None])[0]
    qk_tail = qk_rows[:, (tok - rim) * 2 * key_heads :]
    v_tail = v_in[:, tok - rim :].reshape(prompts, rim * value_heads, DV)
    front = 2 * EDGE - qk_tail.shape[1]
    back = 2 * EDGE - v_tail.shape[1]
    tails = jnp.concatenate(
        [
            jnp.zeros((prompts, front, DK), BF16),
            qk_tail,
            v_tail,
            jnp.zeros((prompts, back, DK), BF16),
        ],
        axis=1,
    )
    halo = lax.ppermute(tails, "seq", [(i, i + 1) for i in range(seq_count - 1)])
    group = value_heads // key_heads
    chips = seq_count // 2
    half = prompts // 2
    jobs = [(head, 0, prompts) for head in range(key_heads)]
    if key_heads == 1:
        jobs = [(0, 0, half), (0, half, prompts - half)]
    total = len(jobs)
    made, finals, sent = [], [], {}
    attended = None
    last = v_in

    def finish(job, results):
        head = jobs[job][0]
        finals.append(results[1])
        if len(results) > 3:
            sent[head] = lax.all_to_all(results[2], "head", 0, 0)
        return results[0], results[-1]

    def earlier(job):
        same = [n for n in range(total) if jobs[n][0] == jobs[job][0]]
        return [finals[n] for n in same[:-1]] if job == same[-1] else None

    def emit(job, entered, attended, last):
        qn, kn, wu, starts, _ = made[job]
        return outputs(
            jobs[job], jobs[job][1:], prompt_lengths, qn, kn, wu, starts, log_decay, write_gain,
            entered, gate_z, norm_gain, key_heads, attended, last,
        )

    for job in jobs:
        mixed = None if job[0] == 0 else made[0][:2]
        wu, starts, own_map, *new = prepare(
            job, prompt_lengths, qk_rows, v_in, halo, qk_taps, conv_v, log_decay, write_gain, key_heads,
            mixed and mixed[1], last,
        )
        last = wu
        moved = [own_map]
        if job == jobs[-1]:
            moved.append(across(own_map, 1))
        else:
            moved += [across(own_map, k) for k in range(1, seq_count)]
        made.append((*(mixed or new), wu, starts, moved))

    entered = []
    for job in range(total - 1):
        results = state_step(placement, group, None, made[job][4], None, earlier(job), last)
        enter, last = finish(job, results)
        entered.append(enter)
    pair = made[-1][4]
    chip_map, last = state_step(placement, group, pair, None, None, None, last)
    chip_maps = [chip_map] + [from_chip_behind(chip_map, k) for k in range(1, chips)]
    for job in range(total - 1):
        attended = last = emit(job, entered[job], attended, last)
    results = state_step(placement, group, None, None, pair + chip_maps, earlier(total - 1), last)
    enter, last = finish(total - 1, results)
    attended = emit(total - 1, enter, attended, last)
    rollout = deliver([sent[head] for head in range(key_heads)])
    return attended, rollout.reshape(1, 1, head_count * value_heads, DK, DV)


def solution(mesh):
    return jax.shard_map(
        shards,
        mesh=mesh,
        in_specs=(
            P(None, "seq", None, "head"),
            P(None, "seq", "head"),
            P(None, "seq", "head"),
            P(None, None, "head"),
            P(None, "head"),
            P(None, "head", "seq"),
            P(None, "head", "seq"),
            P(),
            P(),
            P("seq", None),
        ),
        out_specs=(P(None, "seq", "head"), P("seq", "head", None, None, None)),
        check_vma=False,
    )
```

profile of v0, /device:TPU:0, one launch (start us, length us, event | category | flops | bytes accessed | tf_op | source)
XLA Modules:
  0.0 106.6 jit_solution(2515127895173451490)
XLA Ops:
  0.6 0.7 slice.8
  1.4 0.8 slice.7
  2.2 2.4 %collective-permute-start = (bf16[4,32,128]{2,1,0:T(8,128)(2,1)S(1)}, bf16[4,32,128]{2,1,0:T(8,128)(2,1)S(1)}, u32[]{:S(2)}, u32[]{:S(2)}) collective-permute-start(bf16[4,32,128]{2,1,0:T(8,128)(2,1)S(1)} %pad_maximum_fusion), channel_id=1, source_target_pairs={{0,8},{8,16},{16,24},{1,9},{9,17},{17,25},{2,10},{10,18},{18,26},{... | collective-permute-start | bytes 98312 | tf_op jit(solution)/shard_map/ppermute | solution.py:713
  4.6 0.8 collective-permute-done.refs_2_
  5.4 0.0 copy-start.1
  5.4 0.7 copy-done.1
  6.1 27.4 %prepare.2 = (bf16[4,16,256,128]{3,2,1,0:T(8,128)(2,1)}, bf16[4,2,2048,128]{3,2,1,0:T(8,128)(2,1)}, bf16[8,256,128]{2,1,0:T(8,128)(2,1)S(1)}, bf16[4,1024,256]{2,1,0:T(8,128)(2,1)}, bf16[4,1024,256]{2,1,0:T(8,128)(2,1)}) custom-call(s32[4]{0:T(128)S(1)} %copy-done.1, bf16[4,1024,512]{2,1,0:T(8,128)(2,1)} %refs_1_.3, ...), custom_call_target="tpu_custom_call" | custom-call | flops 20000000000 | bytes 16777216 | tf_op jit(solution)/shard_map/prepare/pallas_call | solution.py:394
  33.4 0.0 collective-permute-start.4
  33.4 4.4 %collective-permute-start.3 = (bf16[8,256,128]{2,1,0:T(8,128)(2,1)S(1)}, bf16[8,256,128]{2,1,0:T(8,128)(2,1)S(1)}, u32[]{:S(2)}, u32[]{:S(2)}) collective-permute-start(bf16[8,256,128]{2,1,0:T(8,128)(2,1)S(1)} %get-tuple-element.24.refs_1_), channel_id=1, source_target_pairs={{0,16},{8,24},{16,0},{24,8},{1,17},{9,25},{17,1},{25,9},{2,18},{10... | collective-permute-start | bytes 1572872 | tf_op jit(solution)/shard_map/ppermute | solution.py:674
  37.8 0.0 collective-permute-start.2
  37.8 0.0 copy-start
  37.8 22.7 %prepare.3 = (bf16[4,16,256,128]{3,2,1,0:T(8,128)(2,1)}, bf16[4,2,2048,128]{3,2,1,0:T(8,128)(2,1)}, bf16[8,256,128]{2,1,0:T(8,128)(2,1)S(1)}) custom-call(s32[4]{0:T(128)S(1)} %copy-done.1, bf16[4,1024,512]{2,1,0:T(8,128)(2,1)} %refs_1_.3, bf16[4,32,128]{2,1,0:T(8,128)(2,1)S(1)} %collective-permute-done.refs_2_, bf16[4,512]{1,0:T(4,128)(2,1)} %refs_3_.3, ...), custom_call_target="tpu_custom_call" | custom-call | flops 20000000000 | bytes 16777216 | tf_op jit(solution)/shard_map/prepare/pallas_call | solution.py:394
  60.6 0.5 collective-permute-start.1
  61.1 0.0 collective-permute-done.4.refs_4_
  61.1 0.0 collective-permute-done.3.refs_3_
  61.1 0.0 collective-permute-done.2.refs_2_
  61.1 0.0 copy-done
  61.1 0.0 copy-start.2
  61.1 2.3 %state_step.3 = (bf16[8,128,128]{2,1,0:T(8,128)(2,1)S(1)}, bf16[8,128,128]{2,1,0:T(8,128)(2,1)}, bf16[8,2,128,128]{3,2,1,0:T(8,128)(2,1)}, f32[8,128]{1,0:T(8,128)}) custom-call(s32[1,8]{1,0:T(1,128)S(1)} %copy-done, bf16[8,256,128]{2,1,0:T(8,128)(2,1)S(1)} %get-tuple-element.24.refs_1_, bf16[8,256,128]{2,1,0:T(8,128)(2,1)S(1)} %collective-permute-done.2.refs_2_, ...), custom_call_target="tpu_custom_call" | custom-call | flops 1000000000 | bytes 1048576 | tf_op jit(solution)/shard_map/state_step/pallas_call | solution.py:641
  63.4 5.8 %all-to-all-start = ((bf16[8,2,128,128]{3,2,1,0:T(8,128)(2,1)}), bf16[8,2,128,128]{3,2,1,0:T(8,128)(2,1)S(1)}, u32[]{:S(2)}, u32[]{:S(2)}) async-start(bf16[8,2,128,128]{3,2,1,0:T(8,128)(2,1)} %get-tuple-element.32), calls=%async_computation | async-start | bytes 1048576 | tf_op jit(solution)/shard_map/all_to_all | solution.py:729
  69.3 0.0 collective-permute-done.1.refs_2_
  69.3 1.4 %state_step.4 = (bf16[8,256,128]{2,1,0:T(8,128)(2,1)S(1)}, f32[8,128]{1,0:T(8,128)}) custom-call(s32[1,8]{1,0:T(1,128)S(1)} %copy-done, bf16[8,256,128]{2,1,0:T(8,128)(2,1)S(1)} %get-tuple-element.23.refs_1_, bf16[8,256,128]{2,1,0:T(8,128)(2,1)S(1)} %collective-permute-done.1.refs_2_, f32[8,128]{1,0:T(8,128)} %get-tuple-element.25.refs_3_), custom_call_target="tpu_custom_call" | custom-call | flops 1000000000 | bytes 1048576 | tf_op jit(solution)/shard_map/state_step/pallas_call | solution.py:641
  70.7 0.0 collective-permute-start.5
  70.7 0.0 copy-done.2
  70.7 11.8 %outputs.2.refs_5_.held_ref = bf16[4,1024,512]{2,1,0:T(8,128)(2,1)} custom-call(s32[4]{0:T(128)S(1)} %copy-done.2, bf16[4,1024,256]{2,1,0:T(8,128)(2,1)} %get-tuple-element.18.qn_ref, bf16[4,1024,256]{2,1,0:T(8,128)(2,1)} %get-tuple-element.19.refs_7_.kn_ref, bf16[4,16,256,128]{3,2,1,0:T(8,128)(2,1)} %get-tuple-element.20.refs_6_.wu_ref, ...), custom_call_target="tpu_custom_call" | custom-call | flops 12000000000 | bytes 16777216 | tf_op jit(solution)/shard_map/outputs/pallas_call | solution.py:489
  82.5 1.8 %collective-permute-done.5.refs_4_ = bf16[8,256,128]{2,1,0:T(8,128)(2,1)S(1)} collective-permute-done((bf16[8,256,128]{2,1,0:T(8,128)(2,1)S(1)}, bf16[8,256,128]{2,1,0:T(8,128)(2,1)S(1)}, u32[]{:S(2)}, u32[]{:S(2)}) %collective-permute-start.5) | collective-permute-done | bytes 524320 | tf_op jit(solution)/shard_map/ppermute | solution.py:681
  84.2 2.1 %state_step.5 = (bf16[8,128,128]{2,1,0:T(8,128)(2,1)S(1)}, bf16[8,128,128]{2,1,0:T(8,128)(2,1)}, bf16[8,2,128,128]{3,2,1,0:T(8,128)(2,1)}, f32[8,128]{1,0:T(8,128)}) custom-call(s32[1,8]{1,0:T(1,128)S(1)} %copy-done, bf16[8,256,128]{2,1,0:T(8,128)(2,1)S(1)} %get-tuple-element.23.refs_1_, bf16[8,256,128]{2,1,0:T(8,128)(2,1)S(1)} %collective-permute-done.1.refs_2_, ...), custom_call_target="tpu_custom_call" | custom-call | flops 1000000000 | bytes 1048576 | tf_op jit(solution)/shard_map/state_step/pallas_call | solution.py:641
  86.3 0.0 all-to-all-done.refs_0_
  86.3 5.7 %all-to-all-start.1 = ((bf16[8,2,128,128]{3,2,1,0:T(8,128)(2,1)}), bf16[8,2,128,128]{3,2,1,0:T(8,128)(2,1)S(1)}, u32[]{:S(2)}, u32[]{:S(2)}) async-start(bf16[8,2,128,128]{3,2,1,0:T(8,128)(2,1)} %get-tuple-element.33), calls=%async_computation.1 | async-start | bytes 1048576 | tf_op jit(solution)/shard_map/all_to_all | solution.py:729
  92.0 11.4 %outputs.3 = bf16[4,1024,512]{2,1,0:T(8,128)(2,1)} custom-call(s32[4]{0:T(128)S(1)} %copy-done.2, bf16[4,1024,256]{2,1,0:T(8,128)(2,1)} %get-tuple-element.18.qn_ref, bf16[4,1024,256]{2,1,0:T(8,128)(2,1)} %get-tuple-element.19.refs_7_.kn_ref, bf16[4,16,256,128]{3,2,1,0:T(8,128)(2,1)} %get-tuple-element.21.refs_5_.wu_ref, ...), custom_call_target="tpu_custom_call", output_to_operand_aliasing={{}: (10, {})} | custom-call | flops 12000000000 | bytes 16777216 | tf_op jit(solution)/shard_map/outputs/pallas_call | solution.py:489
  103.5 1.7 %all-to-all-done.1.refs_1_ = bf16[8,2,128,128]{3,2,1,0:T(8,128)(2,1)S(1)} async-done(((bf16[8,2,128,128]{3,2,1,0:T(8,128)(2,1)}), bf16[8,2,128,128]{3,2,1,0:T(8,128)(2,1)S(1)}, u32[]{:S(2)}, u32[]{:S(2)}) %all-to-all-start.1) | async-done | bytes 524320 | tf_op jit(solution)/shard_map/all_to_all | solution.py:729
  105.2 1.4 %deliver.1 = f32[8,4,128,128]{3,2,1,0:T(8,128)} custom-call(bf16[8,2,128,128]{3,2,1,0:T(8,128)(2,1)S(1)} %all-to-all-done.refs_0_, bf16[8,2,128,128]{3,2,1,0:T(8,128)(2,1)S(1)} %all-to-all-done.1.refs_1_), custom_call_target="tpu_custom_call" | custom-call | tf_op jit(solution)/shard_map/deliver/pallas_call | solution.py:661
  (3 shorter events, 0.0 us)
Async XLA Ops:
  2.2 3.2 %collective-permute-start = (bf16[4,32,128]{2,1,0:T(8,128)(2,1)S(1)}, bf16[4,32,128]{2,1,0:T(8,128)(2,1)S(1)}, u32[]{:S(2)}, u32[]{:S(2)}) collective-permute-start(bf16[4,32,128]{2,1,0:T(8,128)(2,1)S(1)} %pad_maximum_fusion), channel_id=1, source_target_pairs={{0,8},{8,16},{16,24},{1,9},{9,17},{17,25},{2,10},{10,18},{18,26},{... | collective-permute-start | bytes 98312 | tf_op jit(solution)/shard_map/ppermute | solution.py:713
  5.4 0.7 copy-start.1
  33.4 27.7 %collective-permute-start.4 = (bf16[8,256,128]{2,1,0:T(8,128)(2,1)S(1)}, bf16[8,256,128]{2,1,0:T(8,128)(2,1)S(1)}, u32[]{:S(2)}, u32[]{:S(2)}) collective-permute-start(bf16[8,256,128]{2,1,0:T(8,128)(2,1)S(1)} %get-tuple-element.24.refs_1_), channel_id=1, source_target_pairs={{0,24},{8,16},{16,8},{24,0},{1,25},{9,17},{17,9},{25,1},{2,26},{10... | collective-permute-start | bytes 1572872 | tf_op jit(solution)/shard_map/ppermute | solution.py:674
  33.4 27.7 %collective-permute-start.3 = (bf16[8,256,128]{2,1,0:T(8,128)(2,1)S(1)}, bf16[8,256,128]{2,1,0:T(8,128)(2,1)S(1)}, u32[]{:S(2)}, u32[]{:S(2)}) collective-permute-start(bf16[8,256,128]{2,1,0:T(8,128)(2,1)S(1)} %get-tuple-element.24.refs_1_), channel_id=1, source_target_pairs={{0,16},{8,24},{16,0},{24,8},{1,17},{9,25},{17,1},{25,9},{2,18},{10... | collective-permute-start | bytes 1572872 | tf_op jit(solution)/shard_map/ppermute | solution.py:674
  37.8 23.3 %collective-permute-start.2 = (bf16[8,256,128]{2,1,0:T(8,128)(2,1)S(1)}, bf16[8,256,128]{2,1,0:T(8,128)(2,1)S(1)}, u32[]{:S(2)}, u32[]{:S(2)}) collective-permute-start(bf16[8,256,128]{2,1,0:T(8,128)(2,1)S(1)} %get-tuple-element.24.refs_1_), channel_id=1, source_target_pairs={{0,8},{8,0},{16,24},{24,16},{1,9},{9,1},{17,25},{25,17},{2,10},{10... | collective-permute-start | bytes 1572872 | tf_op jit(solution)/shard_map/ppermute | solution.py:674
  37.8 23.3 %copy-start = (s32[1,8]{1,0:T(1,128)S(1)}, s32[1,8]{1,0:T(1,128)}, u32[]{:S(2)}) copy-start(s32[1,8]{1,0:T(1,128)} %refs_0_.9) | copy-start | bytes 100
  60.6 8.7 %collective-permute-start.1 = (bf16[8,256,128]{2,1,0:T(8,128)(2,1)S(1)}, bf16[8,256,128]{2,1,0:T(8,128)(2,1)S(1)}, u32[]{:S(2)}, u32[]{:S(2)}) collective-permute-start(bf16[8,256,128]{2,1,0:T(8,128)(2,1)S(1)} %get-tuple-element.23.refs_1_), channel_id=1, source_target_pairs={{0,8},{8,0},{16,24},{24,16},{1,9},{9,1},{17,25},{25,17},{2,10},{10... | collective-permute-start | bytes 1572872 | tf_op jit(solution)/shard_map/ppermute | solution.py:674
  61.1 9.6 %copy-start.2 = (s32[4]{0:T(128)S(1)}, s32[4]{0:T(128)}, u32[]{:S(2)}) copy-start(s32[4]{0:T(128)} %length_ref.3) | copy-start | bytes 52
  63.4 22.9 %all-to-all-start = ((bf16[8,2,128,128]{3,2,1,0:T(8,128)(2,1)}), bf16[8,2,128,128]{3,2,1,0:T(8,128)(2,1)S(1)}, u32[]{:S(2)}, u32[]{:S(2)}) async-start(bf16[8,2,128,128]{3,2,1,0:T(8,128)(2,1)} %get-tuple-element.32), calls=%async_computation | async-start | bytes 1048576 | tf_op jit(solution)/shard_map/all_to_all | solution.py:729
  70.7 13.6 %collective-permute-start.5 = (bf16[8,256,128]{2,1,0:T(8,128)(2,1)S(1)}, bf16[8,256,128]{2,1,0:T(8,128)(2,1)S(1)}, u32[]{:S(2)}, u32[]{:S(2)}) collective-permute-start(bf16[8,256,128]{2,1,0:T(8,128)(2,1)S(1)} %get-tuple-element.26.refs_3_), channel_id=1, source_target_pairs={{0,16},{8,24},{16,0},{24,8},{1,17},{9,25},{17,1},{25,9},{2,18},{10... | collective-permute-start | bytes 1572872 | tf_op jit(solution)/shard_map/ppermute | solution.py:681
  86.3 18.9 %all-to-all-start.1 = ((bf16[8,2,128,128]{3,2,1,0:T(8,128)(2,1)}), bf16[8,2,128,128]{3,2,1,0:T(8,128)(2,1)S(1)}, u32[]{:S(2)}, u32[]{:S(2)}) async-start(bf16[8,2,128,128]{3,2,1,0:T(8,128)(2,1)} %get-tuple-element.33), calls=%async_computation.1 | async-start | bytes 1048576 | tf_op jit(solution)/shard_map/all_to_all | solution.py:729
where the time goes:
time: 107 us
  Pallas kernels  80.5 us (75%)
  starting transfers between devices  18.8 us (18%)
  waiting for transfers between devices  4.35 us (4%)
  local copies, waits for them, and re-layouts  2.19 us (2%)
    pallas_call x2, Pallas kernels, prepare(): pl.pallas_call(functools.partial(prepare_kernel, first, count, head, grou...  50.1 us
    pallas_call x2, Pallas kernels, outputs(): pl.pallas_call(functools.partial(outputs_kernel, begin, head, group, chun...  23.3 us
    all_to_all x2, starting transfers between devices, finish(): sent[head] = lax.all_to_all(results[2], 'head', 0, 0)  11.5 us
    pallas_call x3, Pallas kernels, state_step(): pl.pallas_call(kernel, in_specs=[pl.BlockSpec(memory_space=pltpu.SMEM)] +...  5.79 us
    ppermute x4, starting transfers between devices, across(): return lax.ppermute(block, 'seq', [(i, i ^ distance) for i in range(count)])  4.9 us
    ppermute x1, starting transfers between devices, shards(): lax.ppermute(tails, 'seq', [(i, i + 1) for i in range(seq_count - 1)])  2.36 us
  transfers between devices with their start and end apart: 8, of which 3 were waited for; matrix products, arithmetic and copies ran while one was open for 0% of the time, Pallas kernels for 49%

commit v1 on v0

--- a/solution.py
+++ b/solution.py
@@ -11,7 +11,7 @@
 DV = 128
 CONV = 4
 BLOCK = 128
-TINY = 16
+TINY = 32
 EDGE = 8
 EPSILON = 1e-06
 VMEM_BYTES = 40 * 1024 * 1024

time: 107 us -> 118 us (1.10)
  Pallas kernels: 80.5 us -> 91.6 us
    pallas_call x2, Pallas kernels: 50.1 us -> 61.3 us  [prepare(): pl.pallas_call(functools.partial(prepare_kernel, first, count, head, grou...]
where the time goes in v1:
time: 118 us
  Pallas kernels  91.6 us (78%)
  starting transfers between devices  18.8 us (16%)
  waiting for transfers between devices  4.35 us (4%)
  local copies, waits for them, and re-layouts  2.19 us (2%)
    pallas_call x2, Pallas kernels, prepare(): pl.pallas_call(functools.partial(prepare_kernel, first, count, head, grou...  61.3 us
    pallas_call x2, Pallas kernels, outputs(): pl.pallas_call(functools.partial(outputs_kernel, begin, head, group, chun...  23.3 us
    all_to_all x2, starting transfers between devices, finish(): sent[head] = lax.all_to_all(results[2], 'head', 0, 0)  11.5 us
    pallas_call x3, Pallas kernels, state_step(): pl.pallas_call(kernel, in_specs=[pl.BlockSpec(memory_space=pltpu.SMEM)] +...  5.62 us
    ppermute x4, starting transfers between devices, across(): return lax.ppermute(block, 'seq', [(i, i ^ distance) for i in range(count)])  4.9 us
  transfers between devices with their start and end apart: 8, of which 3 were waited for; matrix products, arithmetic and copies ran while one was open for 0% of the time, Pallas kernels for 49%

profile of v1, /device:TPU:0, one launch (start us, length us, event | category | flops | bytes accessed | tf_op | source)
XLA Modules:
  0.0 117.6 jit_solution(3409407220874493601)
XLA Ops:
  0.6 0.7 slice.8
  1.4 0.8 slice.7
  2.2 2.4 %collective-permute-start = (bf16[4,32,128]{2,1,0:T(8,128)(2,1)S(1)}, bf16[4,32,128]{2,1,0:T(8,128)(2,1)S(1)}, u32[]{:S(2)}, u32[]{:S(2)}) collective-permute-start(bf16[4,32,128]{2,1,0:T(8,128)(2,1)S(1)} %pad_maximum_fusion), channel_id=1, source_target_pairs={{0,8},{8,16},{16,24},{1,9},{9,17},{17,25},{2,10},{10,18},{18,26},{... | collective-permute-start | bytes 98312 | tf_op jit(solution)/shard_map/ppermute | solution.py:713
  4.6 0.8 collective-permute-done.refs_2_
  5.4 0.0 copy-start.1
  5.4 0.7 copy-done.1
  6.1 32.9 %prepare.2 = (bf16[4,16,256,128]{3,2,1,0:T(8,128)(2,1)}, bf16[4,2,2048,128]{3,2,1,0:T(8,128)(2,1)}, bf16[8,256,128]{2,1,0:T(8,128)(2,1)S(1)}, bf16[4,1024,256]{2,1,0:T(8,128)(2,1)}, bf16[4,1024,256]{2,1,0:T(8,128)(2,1)}) custom-call(s32[4]{0:T(128)S(1)} %copy-done.1, bf16[4,1024,512]{2,1,0:T(8,128)(2,1)} %refs_1_.3, ...), custom_call_target="tpu_custom_call" | custom-call | flops 20000000000 | bytes 16777216 | tf_op jit(solution)/shard_map/prepare/pallas_call | solution.py:394
  39.0 0.0 collective-permute-start.4
  39.0 4.4 %collective-permute-start.3 = (bf16[8,256,128]{2,1,0:T(8,128)(2,1)S(1)}, bf16[8,256,128]{2,1,0:T(8,128)(2,1)S(1)}, u32[]{:S(2)}, u32[]{:S(2)}) collective-permute-start(bf16[8,256,128]{2,1,0:T(8,128)(2,1)S(1)} %get-tuple-element.24.refs_1_), channel_id=1, source_target_pairs={{0,16},{8,24},{16,0},{24,8},{1,17},{9,25},{17,1},{25,9},{2,18},{10... | collective-permute-start | bytes 1572872 | tf_op jit(solution)/shard_map/ppermute | solution.py:674
  43.4 0.0 collective-permute-start.2
  43.4 0.0 copy-start
  43.4 28.4 %prepare.3 = (bf16[4,16,256,128]{3,2,1,0:T(8,128)(2,1)}, bf16[4,2,2048,128]{3,2,1,0:T(8,128)(2,1)}, bf16[8,256,128]{2,1,0:T(8,128)(2,1)S(1)}) custom-call(s32[4]{0:T(128)S(1)} %copy-done.1, bf16[4,1024,512]{2,1,0:T(8,128)(2,1)} %refs_1_.3, bf16[4,32,128]{2,1,0:T(8,128)(2,1)S(1)} %collective-permute-done.refs_2_, bf16[4,512]{1,0:T(4,128)(2,1)} %refs_3_.3, ...), custom_call_target="tpu_custom_call" | custom-call | flops 20000000000 | bytes 16777216 | tf_op jit(solution)/shard_map/prepare/pallas_call | solution.py:394
  71.8 0.5 collective-permute-start.1
  72.3 0.0 collective-permute-done.4.refs_4_
  72.3 0.0 collective-permute-done.3.refs_3_
  72.3 0.0 collective-permute-done.2.refs_2_
  72.3 0.0 copy-done
  72.3 0.0 copy-start.2
  72.3 2.2 %state_step.3 = (bf16[8,128,128]{2,1,0:T(8,128)(2,1)S(1)}, bf16[8,128,128]{2,1,0:T(8,128)(2,1)}, bf16[8,2,128,128]{3,2,1,0:T(8,128)(2,1)}, f32[8,128]{1,0:T(8,128)}) custom-call(s32[1,8]{1,0:T(1,128)S(1)} %copy-done, bf16[8,256,128]{2,1,0:T(8,128)(2,1)S(1)} %get-tuple-element.24.refs_1_, bf16[8,256,128]{2,1,0:T(8,128)(2,1)S(1)} %collective-permute-done.2.refs_2_, ...), custom_call_target="tpu_custom_call" | custom-call | flops 1000000000 | bytes 1048576 | tf_op jit(solution)/shard_map/state_step/pallas_call | solution.py:641
  74.5 5.8 %all-to-all-start = ((bf16[8,2,128,128]{3,2,1,0:T(8,128)(2,1)}), bf16[8,2,128,128]{3,2,1,0:T(8,128)(2,1)S(1)}, u32[]{:S(2)}, u32[]{:S(2)}) async-start(bf16[8,2,128,128]{3,2,1,0:T(8,128)(2,1)} %get-tuple-element.32), calls=%async_computation | async-start | bytes 1048576 | tf_op jit(solution)/shard_map/all_to_all | solution.py:729
  80.3 0.0 collective-permute-done.1.refs_2_
  80.3 1.4 %state_step.4 = (bf16[8,256,128]{2,1,0:T(8,128)(2,1)S(1)}, f32[8,128]{1,0:T(8,128)}) custom-call(s32[1,8]{1,0:T(1,128)S(1)} %copy-done, bf16[8,256,128]{2,1,0:T(8,128)(2,1)S(1)} %get-tuple-element.23.refs_1_, bf16[8,256,128]{2,1,0:T(8,128)(2,1)S(1)} %collective-permute-done.1.refs_2_, f32[8,128]{1,0:T(8,128)} %get-tuple-element.25.refs_3_), custom_call_target="tpu_custom_call" | custom-call | flops 1000000000 | bytes 1048576 | tf_op jit(solution)/shard_map/state_step/pallas_call | solution.py:641
  81.7 0.0 collective-permute-start.5
  81.7 0.0 copy-done.2
  81.7 11.8 %outputs.2.refs_5_.held_ref = bf16[4,1024,512]{2,1,0:T(8,128)(2,1)} custom-call(s32[4]{0:T(128)S(1)} %copy-done.2, bf16[4,1024,256]{2,1,0:T(8,128)(2,1)} %get-tuple-element.18.qn_ref, bf16[4,1024,256]{2,1,0:T(8,128)(2,1)} %get-tuple-element.19.refs_7_.kn_ref, bf16[4,16,256,128]{3,2,1,0:T(8,128)(2,1)} %get-tuple-element.20.refs_6_.wu_ref, ...), custom_call_target="tpu_custom_call" | custom-call | flops 12000000000 | bytes 16777216 | tf_op jit(solution)/shard_map/outputs/pallas_call | solution.py:489
  93.5 1.7 %collective-permute-done.5.refs_4_ = bf16[8,256,128]{2,1,0:T(8,128)(2,1)S(1)} collective-permute-done((bf16[8,256,128]{2,1,0:T(8,128)(2,1)S(1)}, bf16[8,256,128]{2,1,0:T(8,128)(2,1)S(1)}, u32[]{:S(2)}, u32[]{:S(2)}) %collective-permute-start.5) | collective-permute-done | bytes 524320 | tf_op jit(solution)/shard_map/ppermute | solution.py:681
  95.3 2.1 %state_step.5 = (bf16[8,128,128]{2,1,0:T(8,128)(2,1)S(1)}, bf16[8,128,128]{2,1,0:T(8,128)(2,1)}, bf16[8,2,128,128]{3,2,1,0:T(8,128)(2,1)}, f32[8,128]{1,0:T(8,128)}) custom-call(s32[1,8]{1,0:T(1,128)S(1)} %copy-done, bf16[8,256,128]{2,1,0:T(8,128)(2,1)S(1)} %get-tuple-element.23.refs_1_, bf16[8,256,128]{2,1,0:T(8,128)(2,1)S(1)} %collective-permute-done.1.refs_2_, ...), custom_call_target="tpu_custom_call" | custom-call | flops 1000000000 | bytes 1048576 | tf_op jit(solution)/shard_map/state_step/pallas_call | solution.py:641
  97.4 0.0 all-to-all-done.refs_0_
  97.4 5.7 %all-to-all-start.1 = ((bf16[8,2,128,128]{3,2,1,0:T(8,128)(2,1)}), bf16[8,2,128,128]{3,2,1,0:T(8,128)(2,1)S(1)}, u32[]{:S(2)}, u32[]{:S(2)}) async-start(bf16[8,2,128,128]{3,2,1,0:T(8,128)(2,1)} %get-tuple-element.33), calls=%async_computation.1 | async-start | bytes 1048576 | tf_op jit(solution)/shard_map/all_to_all | solution.py:729
  103.1 11.4 %outputs.3 = bf16[4,1024,512]{2,1,0:T(8,128)(2,1)} custom-call(s32[4]{0:T(128)S(1)} %copy-done.2, bf16[4,1024,256]{2,1,0:T(8,128)(2,1)} %get-tuple-element.18.qn_ref, bf16[4,1024,256]{2,1,0:T(8,128)(2,1)} %get-tuple-element.19.refs_7_.kn_ref, bf16[4,16,256,128]{3,2,1,0:T(8,128)(2,1)} %get-tuple-element.21.refs_5_.wu_ref, ...), custom_call_target="tpu_custom_call", output_to_operand_aliasing={{}: (10, {})} | custom-call | flops 12000000000 | bytes 16777216 | tf_op jit(solution)/shard_map/outputs/pallas_call | solution.py:489
  114.5 1.8 %all-to-all-done.1.refs_1_ = bf16[8,2,128,128]{3,2,1,0:T(8,128)(2,1)S(1)} async-done(((bf16[8,2,128,128]{3,2,1,0:T(8,128)(2,1)}), bf16[8,2,128,128]{3,2,1,0:T(8,128)(2,1)S(1)}, u32[]{:S(2)}, u32[]{:S(2)}) %all-to-all-start.1) | async-done | bytes 524320 | tf_op jit(solution)/shard_map/all_to_all | solution.py:729
  116.3 1.4 %deliver.1 = f32[8,4,128,128]{3,2,1,0:T(8,128)} custom-call(bf16[8,2,128,128]{3,2,1,0:T(8,128)(2,1)S(1)} %all-to-all-done.refs_0_, bf16[8,2,128,128]{3,2,1,0:T(8,128)(2,1)S(1)} %all-to-all-done.1.refs_1_), custom_call_target="tpu_custom_call" | custom-call | tf_op jit(solution)/shard_map/deliver/pallas_call | solution.py:661
  (3 shorter events, 0.0 us)
Async XLA Ops:
  2.2 3.2 %collective-permute-start = (bf16[4,32,128]{2,1,0:T(8,128)(2,1)S(1)}, bf16[4,32,128]{2,1,0:T(8,128)(2,1)S(1)}, u32[]{:S(2)}, u32[]{:S(2)}) collective-permute-start(bf16[4,32,128]{2,1,0:T(8,128)(2,1)S(1)} %pad_maximum_fusion), channel_id=1, source_target_pairs={{0,8},{8,16},{16,24},{1,9},{9,17},{17,25},{2,10},{10,18},{18,26},{... | collective-permute-start | bytes 98312 | tf_op jit(solution)/shard_map/ppermute | solution.py:713
  5.4 0.7 copy-start.1
  39.0 33.3 %collective-permute-start.4 = (bf16[8,256,128]{2,1,0:T(8,128)(2,1)S(1)}, bf16[8,256,128]{2,1,0:T(8,128)(2,1)S(1)}, u32[]{:S(2)}, u32[]{:S(2)}) collective-permute-start(bf16[8,256,128]{2,1,0:T(8,128)(2,1)S(1)} %get-tuple-element.24.refs_1_), channel_id=1, source_target_pairs={{0,24},{8,16},{16,8},{24,0},{1,25},{9,17},{17,9},{25,1},{2,26},{10... | collective-permute-start | bytes 1572872 | tf_op jit(solution)/shard_map/ppermute | solution.py:674
  39.0 33.3 %collective-permute-start.3 = (bf16[8,256,128]{2,1,0:T(8,128)(2,1)S(1)}, bf16[8,256,128]{2,1,0:T(8,128)(2,1)S(1)}, u32[]{:S(2)}, u32[]{:S(2)}) collective-permute-start(bf16[8,256,128]{2,1,0:T(8,128)(2,1)S(1)} %get-tuple-element.24.refs_1_), channel_id=1, source_target_pairs={{0,16},{8,24},{16,0},{24,8},{1,17},{9,25},{17,1},{25,9},{2,18},{10... | collective-permute-start | bytes 1572872 | tf_op jit(solution)/shard_map/ppermute | solution.py:674
  43.4 28.9 %collective-permute-start.2 = (bf16[8,256,128]{2,1,0:T(8,128)(2,1)S(1)}, bf16[8,256,128]{2,1,0:T(8,128)(2,1)S(1)}, u32[]{:S(2)}, u32[]{:S(2)}) collective-permute-start(bf16[8,256,128]{2,1,0:T(8,128)(2,1)S(1)} %get-tuple-element.24.refs_1_), channel_id=1, source_target_pairs={{0,8},{8,0},{16,24},{24,16},{1,9},{9,1},{17,25},{25,17},{2,10},{10... | collective-permute-start | bytes 1572872 | tf_op jit(solution)/shard_map/ppermute | solution.py:674
  43.4 28.9 %copy-start = (s32[1,8]{1,0:T(1,128)S(1)}, s32[1,8]{1,0:T(1,128)}, u32[]{:S(2)}) copy-start(s32[1,8]{1,0:T(1,128)} %refs_0_.9) | copy-start | bytes 100
  71.8 8.5 %collective-permute-start.1 = (bf16[8,256,128]{2,1,0:T(8,128)(2,1)S(1)}, bf16[8,256,128]{2,1,0:T(8,128)(2,1)S(1)}, u32[]{:S(2)}, u32[]{:S(2)}) collective-permute-start(bf16[8,256,128]{2,1,0:T(8,128)(2,1)S(1)} %get-tuple-element.23.refs_1_), channel_id=1, source_target_pairs={{0,8},{8,0},{16,24},{24,16},{1,9},{9,1},{17,25},{25,17},{2,10},{10... | collective-permute-start | bytes 1572872 | tf_op jit(solution)/shard_map/ppermute | solution.py:674
  72.3 9.4 %copy-start.2 = (s32[4]{0:T(128)S(1)}, s32[4]{0:T(128)}, u32[]{:S(2)}) copy-start(s32[4]{0:T(128)} %length_ref.3) | copy-start | bytes 52
  74.5 22.9 %all-to-all-start = ((bf16[8,2,128,128]{3,2,1,0:T(8,128)(2,1)}), bf16[8,2,128,128]{3,2,1,0:T(8,128)(2,1)S(1)}, u32[]{:S(2)}, u32[]{:S(2)}) async-start(bf16[8,2,128,128]{3,2,1,0:T(8,128)(2,1)} %get-tuple-element.32), calls=%async_computation | async-start | bytes 1048576 | tf_op jit(solution)/shard_map/all_to_all | solution.py:729
  81.7 13.6 %collective-permute-start.5 = (bf16[8,256,128]{2,1,0:T(8,128)(2,1)S(1)}, bf16[8,256,128]{2,1,0:T(8,128)(2,1)S(1)}, u32[]{:S(2)}, u32[]{:S(2)}) collective-permute-start(bf16[8,256,128]{2,1,0:T(8,128)(2,1)S(1)} %get-tuple-element.26.refs_3_), channel_id=1, source_target_pairs={{0,16},{8,24},{16,0},{24,8},{1,17},{9,25},{17,1},{25,9},{2,18},{10... | collective-permute-start | bytes 1572872 | tf_op jit(solution)/shard_map/ppermute | solution.py:681
  97.4 18.9 %all-to-all-start.1 = ((bf16[8,2,128,128]{3,2,1,0:T(8,128)(2,1)}), bf16[8,2,128,128]{3,2,1,0:T(8,128)(2,1)S(1)}, u32[]{:S(2)}, u32[]{:S(2)}) async-start(bf16[8,2,128,128]{3,2,1,0:T(8,128)(2,1)} %get-tuple-element.33), calls=%async_computation.1 | async-start | bytes 1048576 | tf_op jit(solution)/shard_map/all_to_all | solution.py:729

commit v2 on v0

--- a/solution.py
+++ b/solution.py
@@ -12,6 +12,8 @@
 CONV = 4
 BLOCK = 128
 TINY = 16
+ROWS = 8
+STRIDE = 4
 EDGE = 8
 EPSILON = 1e-06
 VMEM_BYTES = 40 * 1024 * 1024
@@ -119,6 +121,11 @@
             to_ref[0, span, kind // 2 * DK : (kind // 2 + 1) * DK] = rows.astype(BF16)
 
 
+def one_row(tiles, j):
+    tile = tiles[j // ROWS]
+    return jnp.broadcast_to(tile[j % ROWS : j % ROWS + 1], tile.shape)
+
+
 def weave(*lists):
     places = []
     for which, entries in enumerate(lists):
@@ -221,6 +228,7 @@
         small_row = lax.broadcasted_iota(jnp.int32, (TINY, BLOCK), 0)
         small_lane = lax.broadcasted_iota(jnp.int32, (TINY, BLOCK), 1)
         part_of = small_lane // TINY
+        lane_part = part_of[:ROWS]
         tiny_eye = jnp.where(small_row == small_lane % TINY, 1.0, 0.0).astype(F32)
 
         keys = [kn_ref[0, span(c), key_columns] for c in range(chunks)]
@@ -242,16 +250,30 @@
                 tiny = strict[0:TINY]
                 for b in range(1, BLOCK // TINY):
                     tiny = jnp.where(part_of == b, strict[b * TINY : (b + 1) * TINY], tiny)
-                compact[r] = tiny
-                solved[r] = tiny_eye
-
-            def eliminate(j, r):
-                factor = jnp.take_along_axis(compact[r], part_of * TINY + j, axis=1, mode="promise_in_bounds")
-                solved[r] = solved[r] + factor * solved[r][j : j + 1, :]
+                compact[r] = [tiny[t : t + ROWS] for t in range(0, TINY, ROWS)]
+                solved[r] = [tiny_eye[t : t + ROWS] for t in range(0, TINY, ROWS)]
+
+            def eliminate(last, r):
+                group_rows = range(last, max(last - STRIDE, 0), -1)
+                factor, taken = {}, {}
+                for j in group_rows:
+                    pick = lane_part * TINY + j
+                    factor[j] = [
+                        jnp.take_along_axis(tile, pick, axis=1, mode="promise_in_bounds")
+                        for tile in compact[r][: j // ROWS + 1]
+                    ]
+                    taken[j] = one_row(solved[r], j)
+                for j in group_rows:
+                    for i in range(last, j, -1):
+                        taken[j] = taken[j] + one_row(factor[i], j) * taken[i]
+                for j in group_rows:
+                    for t, tile in enumerate(factor[j]):
+                        solved[r][t] = solved[r][t] + tile * taken[j]
 
             def place(r):
+                whole = jnp.concatenate(solved[r], axis=0)
                 for b in range(BLOCK // TINY):
-                    x_scr[r, b * TINY : (b + 1) * TINY, :] = jnp.where(part_of == b, solved[r], 0.0).astype(BF16)
+                    x_scr[r, b * TINY : (b + 1) * TINY, :] = jnp.where(part_of == b, whole, 0.0).astype(BF16)
 
             def convolve(c):
                 mixed[c] = mixed_rows(v_pad, v_taps, EDGE, 0, 1, c).astype(BF16)
@@ -266,9 +288,9 @@
                 ops.append(functools.partial(start, c))
             for h, c in local:
                 ops.append(functools.partial(mask, h, c))
-            for j in range(TINY - 1, 0, -1):
+            for last in range(TINY - 1, 0, -STRIDE):
                 for h, c in local:
-                    ops.append(functools.partial(eliminate, j, h * chunks + c))
+                    ops.append(functools.partial(eliminate, last, h * chunks + c))
             for h, c in local:
                 ops.append(functools.partial(place, h * chunks + c))
             right = []

time: 107 us -> 108 us (level)
  Pallas kernels: 80.5 us -> 81.9 us
    pallas_call x2, Pallas kernels: 50.1 us -> 51.4 us  [prepare(): pl.pallas_call(functools.partial(prepare_kernel, first, count, head, grou...]
  transfers between devices with their start and end apart: 8 -> 8, of which waited for: 3 -> 3; matrix products, arithmetic and copies ran while one was open for 0% -> 0% of each run, Pallas kernels for 49% -> 48%
where the time goes in v2:
time: 108 us
  Pallas kernels  81.9 us (76%)
  starting transfers between devices  18.8 us (17%)
  waiting for transfers between devices  4.35 us (4%)
  local copies, waits for them, and re-layouts  2.19 us (2%)
    pallas_call x2, Pallas kernels, prepare(): pl.pallas_call(functools.partial(prepare_kernel, first, count, head, grou...  51.4 us
    pallas_call x2, Pallas kernels, outputs(): pl.pallas_call(functools.partial(outputs_kernel, begin, head, group, chun...  23.3 us
    all_to_all x2, starting transfers between devices, finish(): sent[head] = lax.all_to_all(results[2], 'head', 0, 0)  11.5 us
    pallas_call x3, Pallas kernels, state_step(): pl.pallas_call(kernel, in_specs=[pl.BlockSpec(memory_space=pltpu.SMEM)] +...  5.79 us
    ppermute x4, starting transfers between devices, across(): return lax.ppermute(block, 'seq', [(i, i ^ distance) for i in range(count)])  4.9 us
    ppermute x1, starting transfers between devices, shards(): lax.ppermute(tails, 'seq', [(i, i + 1) for i in range(seq_count - 1)])  2.36 us
  transfers between devices with their start and end apart: 8, of which 3 were waited for; matrix products, arithmetic and copies ran while one was open for 0% of the time, Pallas kernels for 48%

profile of v2, /device:TPU:0, one launch (start us, length us, event | category | flops | bytes accessed | tf_op | source)
XLA Modules:
  0.0 107.9 jit_solution(16093007855113708630)
XLA Ops:
  0.6 0.7 slice.8
  1.4 0.8 slice.7
  2.2 2.4 %collective-permute-start = (bf16[4,32,128]{2,1,0:T(8,128)(2,1)S(1)}, bf16[4,32,128]{2,1,0:T(8,128)(2,1)S(1)}, u32[]{:S(2)}, u32[]{:S(2)}) collective-permute-start(bf16[4,32,128]{2,1,0:T(8,128)(2,1)S(1)} %pad_maximum_fusion), channel_id=1, source_target_pairs={{0,8},{8,16},{16,24},{1,9},{9,17},{17,25},{2,10},{10,18},{18,26},{... | collective-permute-start | bytes 98312 | tf_op jit(solution)/shard_map/ppermute | solution.py:735
  4.6 0.8 collective-permute-done.refs_2_
  5.4 0.0 copy-start.1
  5.4 0.7 copy-done.1
  6.1 28.3 %prepare.2 = (bf16[4,16,256,128]{3,2,1,0:T(8,128)(2,1)}, bf16[4,2,2048,128]{3,2,1,0:T(8,128)(2,1)}, bf16[8,256,128]{2,1,0:T(8,128)(2,1)S(1)}, bf16[4,1024,256]{2,1,0:T(8,128)(2,1)}, bf16[4,1024,256]{2,1,0:T(8,128)(2,1)}) custom-call(s32[4]{0:T(128)S(1)} %copy-done.1, bf16[4,1024,512]{2,1,0:T(8,128)(2,1)} %refs_1_.3, ...), custom_call_target="tpu_custom_call" | custom-call | flops 20000000000 | bytes 16777216 | tf_op jit(solution)/shard_map/prepare/pallas_call | solution.py:416
  34.4 0.0 collective-permute-start.4
  34.4 4.4 %collective-permute-start.3 = (bf16[8,256,128]{2,1,0:T(8,128)(2,1)S(1)}, bf16[8,256,128]{2,1,0:T(8,128)(2,1)S(1)}, u32[]{:S(2)}, u32[]{:S(2)}) collective-permute-start(bf16[8,256,128]{2,1,0:T(8,128)(2,1)S(1)} %get-tuple-element.24.refs_1_), channel_id=1, source_target_pairs={{0,16},{8,24},{16,0},{24,8},{1,17},{9,25},{17,1},{25,9},{2,18},{10... | collective-permute-start | bytes 1572872 | tf_op jit(solution)/shard_map/ppermute | solution.py:696
  38.8 0.0 collective-permute-start.2
  38.8 0.0 copy-start
  38.8 23.1 %prepare.3 = (bf16[4,16,256,128]{3,2,1,0:T(8,128)(2,1)}, bf16[4,2,2048,128]{3,2,1,0:T(8,128)(2,1)}, bf16[8,256,128]{2,1,0:T(8,128)(2,1)S(1)}) custom-call(s32[4]{0:T(128)S(1)} %copy-done.1, bf16[4,1024,512]{2,1,0:T(8,128)(2,1)} %refs_1_.3, bf16[4,32,128]{2,1,0:T(8,128)(2,1)S(1)} %collective-permute-done.refs_2_, bf16[4,512]{1,0:T(4,128)(2,1)} %refs_3_.3, ...), custom_call_target="tpu_custom_call" | custom-call | flops 20000000000 | bytes 16777216 | tf_op jit(solution)/shard_map/prepare/pallas_call | solution.py:416
  61.9 0.5 collective-permute-start.1
  62.4 0.0 collective-permute-done.4.refs_4_
  62.4 0.0 collective-permute-done.3.refs_3_
  62.4 0.0 collective-permute-done.2.refs_2_
  62.4 0.0 copy-done
  62.4 0.0 copy-start.2
  62.4 2.3 %state_step.3 = (bf16[8,128,128]{2,1,0:T(8,128)(2,1)S(1)}, bf16[8,128,128]{2,1,0:T(8,128)(2,1)}, bf16[8,2,128,128]{3,2,1,0:T(8,128)(2,1)}, f32[8,128]{1,0:T(8,128)}) custom-call(s32[1,8]{1,0:T(1,128)S(1)} %copy-done, bf16[8,256,128]{2,1,0:T(8,128)(2,1)S(1)} %get-tuple-element.24.refs_1_, bf16[8,256,128]{2,1,0:T(8,128)(2,1)S(1)} %collective-permute-done.2.refs_2_, ...), custom_call_target="tpu_custom_call" | custom-call | flops 1000000000 | bytes 1048576 | tf_op jit(solution)/shard_map/state_step/pallas_call | solution.py:663
  64.8 5.8 %all-to-all-start = ((bf16[8,2,128,128]{3,2,1,0:T(8,128)(2,1)}), bf16[8,2,128,128]{3,2,1,0:T(8,128)(2,1)S(1)}, u32[]{:S(2)}, u32[]{:S(2)}) async-start(bf16[8,2,128,128]{3,2,1,0:T(8,128)(2,1)} %get-tuple-element.32), calls=%async_computation | async-start | bytes 1048576 | tf_op jit(solution)/shard_map/all_to_all | solution.py:751
  70.6 0.0 collective-permute-done.1.refs_2_
  70.6 1.4 %state_step.4 = (bf16[8,256,128]{2,1,0:T(8,128)(2,1)S(1)}, f32[8,128]{1,0:T(8,128)}) custom-call(s32[1,8]{1,0:T(1,128)S(1)} %copy-done, bf16[8,256,128]{2,1,0:T(8,128)(2,1)S(1)} %get-tuple-element.23.refs_1_, bf16[8,256,128]{2,1,0:T(8,128)(2,1)S(1)} %collective-permute-done.1.refs_2_, f32[8,128]{1,0:T(8,128)} %get-tuple-element.25.refs_3_), custom_call_target="tpu_custom_call" | custom-call | flops 1000000000 | bytes 1048576 | tf_op jit(solution)/shard_map/state_step/pallas_call | solution.py:663
  72.0 0.0 collective-permute-start.5
  72.0 0.0 copy-done.2
  72.0 11.8 %outputs.2.refs_5_.held_ref = bf16[4,1024,512]{2,1,0:T(8,128)(2,1)} custom-call(s32[4]{0:T(128)S(1)} %copy-done.2, bf16[4,1024,256]{2,1,0:T(8,128)(2,1)} %get-tuple-element.18.qn_ref, bf16[4,1024,256]{2,1,0:T(8,128)(2,1)} %get-tuple-element.19.refs_7_.kn_ref, bf16[4,16,256,128]{3,2,1,0:T(8,128)(2,1)} %get-tuple-element.20.refs_6_.wu_ref, ...), custom_call_target="tpu_custom_call" | custom-call | flops 12000000000 | bytes 16777216 | tf_op jit(solution)/shard_map/outputs/pallas_call | solution.py:511
  83.8 1.8 %collective-permute-done.5.refs_4_ = bf16[8,256,128]{2,1,0:T(8,128)(2,1)S(1)} collective-permute-done((bf16[8,256,128]{2,1,0:T(8,128)(2,1)S(1)}, bf16[8,256,128]{2,1,0:T(8,128)(2,1)S(1)}, u32[]{:S(2)}, u32[]{:S(2)}) %collective-permute-start.5) | collective-permute-done | bytes 524320 | tf_op jit(solution)/shard_map/ppermute | solution.py:703
  85.6 2.1 %state_step.5 = (bf16[8,128,128]{2,1,0:T(8,128)(2,1)S(1)}, bf16[8,128,128]{2,1,0:T(8,128)(2,1)}, bf16[8,2,128,128]{3,2,1,0:T(8,128)(2,1)}, f32[8,128]{1,0:T(8,128)}) custom-call(s32[1,8]{1,0:T(1,128)S(1)} %copy-done, bf16[8,256,128]{2,1,0:T(8,128)(2,1)S(1)} %get-tuple-element.23.refs_1_, bf16[8,256,128]{2,1,0:T(8,128)(2,1)S(1)} %collective-permute-done.1.refs_2_, ...), custom_call_target="tpu_custom_call" | custom-call | flops 1000000000 | bytes 1048576 | tf_op jit(solution)/shard_map/state_step/pallas_call | solution.py:663
  87.6 0.0 all-to-all-done.refs_0_
  87.7 5.7 %all-to-all-start.1 = ((bf16[8,2,128,128]{3,2,1,0:T(8,128)(2,1)}), bf16[8,2,128,128]{3,2,1,0:T(8,128)(2,1)S(1)}, u32[]{:S(2)}, u32[]{:S(2)}) async-start(bf16[8,2,128,128]{3,2,1,0:T(8,128)(2,1)} %get-tuple-element.33), calls=%async_computation.1 | async-start | bytes 1048576 | tf_op jit(solution)/shard_map/all_to_all | solution.py:751
  93.4 11.4 %outputs.3 = bf16[4,1024,512]{2,1,0:T(8,128)(2,1)} custom-call(s32[4]{0:T(128)S(1)} %copy-done.2, bf16[4,1024,256]{2,1,0:T(8,128)(2,1)} %get-tuple-element.18.qn_ref, bf16[4,1024,256]{2,1,0:T(8,128)(2,1)} %get-tuple-element.19.refs_7_.kn_ref, bf16[4,16,256,128]{3,2,1,0:T(8,128)(2,1)} %get-tuple-element.21.refs_5_.wu_ref, ...), custom_call_target="tpu_custom_call", output_to_operand_aliasing={{}: (10, {})} | custom-call | flops 12000000000 | bytes 16777216 | tf_op jit(solution)/shard_map/outputs/pallas_call | solution.py:511
  104.8 1.7 %all-to-all-done.1.refs_1_ = bf16[8,2,128,128]{3,2,1,0:T(8,128)(2,1)S(1)} async-done(((bf16[8,2,128,128]{3,2,1,0:T(8,128)(2,1)}), bf16[8,2,128,128]{3,2,1,0:T(8,128)(2,1)S(1)}, u32[]{:S(2)}, u32[]{:S(2)}) %all-to-all-start.1) | async-done | bytes 524320 | tf_op jit(solution)/shard_map/all_to_all | solution.py:751
  106.5 1.4 %deliver.1 = f32[8,4,128,128]{3,2,1,0:T(8,128)} custom-call(bf16[8,2,128,128]{3,2,1,0:T(8,128)(2,1)S(1)} %all-to-all-done.refs_0_, bf16[8,2,128,128]{3,2,1,0:T(8,128)(2,1)S(1)} %all-to-all-done.1.refs_1_), custom_call_target="tpu_custom_call" | custom-call | tf_op jit(solution)/shard_map/deliver/pallas_call | solution.py:683
  (3 shorter events, 0.0 us)
Async XLA Ops:
  2.2 3.2 %collective-permute-start = (bf16[4,32,128]{2,1,0:T(8,128)(2,1)S(1)}, bf16[4,32,128]{2,1,0:T(8,128)(2,1)S(1)}, u32[]{:S(2)}, u32[]{:S(2)}) collective-permute-start(bf16[4,32,128]{2,1,0:T(8,128)(2,1)S(1)} %pad_maximum_fusion), channel_id=1, source_target_pairs={{0,8},{8,16},{16,24},{1,9},{9,17},{17,25},{2,10},{10,18},{18,26},{... | collective-permute-start | bytes 98312 | tf_op jit(solution)/shard_map/ppermute | solution.py:735
  5.4 0.7 copy-start.1
  34.4 28.0 %collective-permute-start.4 = (bf16[8,256,128]{2,1,0:T(8,128)(2,1)S(1)}, bf16[8,256,128]{2,1,0:T(8,128)(2,1)S(1)}, u32[]{:S(2)}, u32[]{:S(2)}) collective-permute-start(bf16[8,256,128]{2,1,0:T(8,128)(2,1)S(1)} %get-tuple-element.24.refs_1_), channel_id=1, source_target_pairs={{0,24},{8,16},{16,8},{24,0},{1,25},{9,17},{17,9},{25,1},{2,26},{10... | collective-permute-start | bytes 1572872 | tf_op jit(solution)/shard_map/ppermute | solution.py:696
  34.4 28.0 %collective-permute-start.3 = (bf16[8,256,128]{2,1,0:T(8,128)(2,1)S(1)}, bf16[8,256,128]{2,1,0:T(8,128)(2,1)S(1)}, u32[]{:S(2)}, u32[]{:S(2)}) collective-permute-start(bf16[8,256,128]{2,1,0:T(8,128)(2,1)S(1)} %get-tuple-element.24.refs_1_), channel_id=1, source_target_pairs={{0,16},{8,24},{16,0},{24,8},{1,17},{9,25},{17,1},{25,9},{2,18},{10... | collective-permute-start | bytes 1572872 | tf_op jit(solution)/shard_map/ppermute | solution.py:696
  38.8 23.6 %collective-permute-start.2 = (bf16[8,256,128]{2,1,0:T(8,128)(2,1)S(1)}, bf16[8,256,128]{2,1,0:T(8,128)(2,1)S(1)}, u32[]{:S(2)}, u32[]{:S(2)}) collective-permute-start(bf16[8,256,128]{2,1,0:T(8,128)(2,1)S(1)} %get-tuple-element.24.refs_1_), channel_id=1, source_target_pairs={{0,8},{8,0},{16,24},{24,16},{1,9},{9,1},{17,25},{25,17},{2,10},{10... | collective-permute-start | bytes 1572872 | tf_op jit(solution)/shard_map/ppermute | solution.py:696
  38.8 23.6 %copy-start = (s32[1,8]{1,0:T(1,128)S(1)}, s32[1,8]{1,0:T(1,128)}, u32[]{:S(2)}) copy-start(s32[1,8]{1,0:T(1,128)} %refs_0_.9) | copy-start | bytes 100
  61.9 8.7 %collective-permute-start.1 = (bf16[8,256,128]{2,1,0:T(8,128)(2,1)S(1)}, bf16[8,256,128]{2,1,0:T(8,128)(2,1)S(1)}, u32[]{:S(2)}, u32[]{:S(2)}) collective-permute-start(bf16[8,256,128]{2,1,0:T(8,128)(2,1)S(1)} %get-tuple-element.23.refs_1_), channel_id=1, source_target_pairs={{0,8},{8,0},{16,24},{24,16},{1,9},{9,1},{17,25},{25,17},{2,10},{10... | collective-permute-start | bytes 1572872 | tf_op jit(solution)/shard_map/ppermute | solution.py:696
  62.4 9.6 %copy-start.2 = (s32[4]{0:T(128)S(1)}, s32[4]{0:T(128)}, u32[]{:S(2)}) copy-start(s32[4]{0:T(128)} %length_ref.3) | copy-start | bytes 52
  64.8 22.9 %all-to-all-start = ((bf16[8,2,128,128]{3,2,1,0:T(8,128)(2,1)}), bf16[8,2,128,128]{3,2,1,0:T(8,128)(2,1)S(1)}, u32[]{:S(2)}, u32[]{:S(2)}) async-start(bf16[8,2,128,128]{3,2,1,0:T(8,128)(2,1)} %get-tuple-element.32), calls=%async_computation | async-start | bytes 1048576 | tf_op jit(solution)/shard_map/all_to_all | solution.py:751
  72.0 13.6 %collective-permute-start.5 = (bf16[8,256,128]{2,1,0:T(8,128)(2,1)S(1)}, bf16[8,256,128]{2,1,0:T(8,128)(2,1)S(1)}, u32[]{:S(2)}, u32[]{:S(2)}) collective-permute-start(bf16[8,256,128]{2,1,0:T(8,128)(2,1)S(1)} %get-tuple-element.26.refs_3_), channel_id=1, source_target_pairs={{0,16},{8,24},{16,0},{24,8},{1,17},{9,25},{17,1},{25,9},{2,18},{10... | collective-permute-start | bytes 1572872 | tf_op jit(solution)/shard_map/ppermute | solution.py:703
  87.7 18.9 %all-to-all-start.1 = ((bf16[8,2,128,128]{3,2,1,0:T(8,128)(2,1)}), bf16[8,2,128,128]{3,2,1,0:T(8,128)(2,1)S(1)}, u32[]{:S(2)}, u32[]{:S(2)}) async-start(bf16[8,2,128,128]{3,2,1,0:T(8,128)(2,1)} %get-tuple-element.33), calls=%async_computation.1 | async-start | bytes 1048576 | tf_op jit(solution)/shard_map/all_to_all | solution.py:751

commit v3 on v0

--- a/solution.py
+++ b/solution.py
@@ -14,7 +14,7 @@
 TINY = 16
 EDGE = 8
 EPSILON = 1e-06
-VMEM_BYTES = 40 * 1024 * 1024
+VMEM_BYTES = 24 * 1024 * 1024
 SMALL_VMEM_BYTES = 8 * 1024 * 1024
 F32 = jnp.float32
 BF16 = jnp.bfloat16
@@ -131,14 +131,15 @@
     length_ref, v_ref, halo_ref, v_taps_ref, log_ref, gain_ref, after_ref = refs[:7]
     refs = refs[7:]
     if mixes:
-        qk_ref, qk_taps_ref, wu_ref, start_ref, map_ref, qn_ref, kn_ref = refs[:7]
-        v_pad, m_scr, b_scr, fade_scr, st_scr, a_scr, x_scr, y_scr, raw_scr = refs[7:]
+        qk_ref, qk_taps_ref, wu_ref, start_ref, map_ref, token_ref, qn_ref, kn_ref = refs[:8]
+        v_pad, m_scr, b_scr, fade_scr, st_scr, a_scr, x_scr, y_scr, raw_scr = refs[8:]
         key_columns = slice(head * DK, (head + 1) * DK)
     else:
-        kn_ref, wu_ref, start_ref, map_ref = refs[:4]
-        v_pad, m_scr, b_scr, fade_scr, st_scr, a_scr, x_scr, y_scr = refs[4:]
+        kn_ref, wu_ref, start_ref, map_ref, token_ref = refs[:5]
+        v_pad, m_scr, b_scr, fade_scr, st_scr, a_scr, x_scr, y_scr = refs[5:]
         key_columns = slice(0, DK)
     step = pl.program_id(0)
+    token_ref[...] = jnp.zeros_like(token_ref)
     used = length_ref[first + jnp.minimum(step, count - 1)] - lax.axis_index("seq") * (chunks * BLOCK)
     units = [(h, c) for c in range(chunks) for h in range(group)]
     slot = step % 2
@@ -210,7 +211,7 @@
 
         cum, gain = gates_of_heads(log_ref, gain_ref, used, head, group)
         both_gains = gain * jnp.exp(cum)
-        columns = as_columns(jnp.concatenate([cum] * (8 // group), axis=0), chunks)
+        bases = block_bases([-cum], chunks)
 
         def span(c):
             return slice(c * BLOCK, (c + 1) * BLOCK)
@@ -227,17 +228,17 @@
         turned = {}
 
         def front(some):
-            ops, kk, compact, solved, mixed = [], {}, {}, {}, {}
+            ops, kk, later, compact, solved, mixed = [], {}, {}, {}, {}, {}
             local = [(h, c) for c in some for h in range(group)]
 
             def start(c):
                 turned[c] = keys[c].T
                 kk[c] = dot(keys[c], turned[c])
+                later[c] = spread_squares(bases[c], group, 1)
 
             def mask(h, c):
                 r = h * chunks + c
-                ratio = jnp.exp(cum[h : h + 1, span(c)] - columns[:, c * 8 + h : c * 8 + h + 1])
-                strict = jnp.where(above, ratio * kk[c] * -gain[h : h + 1, span(c)], 0.0)
+                strict = jnp.where(above, jnp.exp(later[c][h]) * kk[c] * -gain[h : h + 1, span(c)], 0.0)
                 a_scr[r] = strict.astype(BF16)
                 tiny = strict[0:TINY]
                 for b in range(1, BLOCK // TINY):
@@ -363,11 +364,13 @@
         pl.BlockSpec((1, rows, DK + DV, BLOCK), lambda i, lengths: (now(i), 0, 0, 0)),
         pl.BlockSpec((1, group, chunks * (DV + DK), DK), lambda i, lengths: (before(i), 0, 0, 0)),
         pl.BlockSpec((group, DV + DK, DK), lambda i, lengths: (before(i), 0, 0)),
+        pl.BlockSpec((8, 128), lambda i, lengths: (0, 0)),
     ]
     out_shape = [
-        pltpu.HBM((count, rows, DK + DV, BLOCK), BF16),
-        pltpu.HBM((count, group, chunks * (DV + DK), DK), BF16),
+        jax.ShapeDtypeStruct((count, rows, DK + DV, BLOCK), BF16),
+        jax.ShapeDtypeStruct((count, group, chunks * (DV + DK), DK), BF16),
         jax.ShapeDtypeStruct((count * group, DV + DK, DK), BF16),
+        pltpu.HBM((8, 128), F32),
     ]
     scratch = [
         pltpu.VMEM((tok + EDGE, wide), F32),
@@ -386,10 +389,10 @@
             pl.BlockSpec(qk_taps.shape, lambda i, lengths: (0, 0)),
         ]
         out_specs += [pl.BlockSpec((1, tok, key_heads * DK), lambda i, lengths: (now(i), 0, 0))] * 2
-        out_shape += [pltpu.HBM((count, tok, key_heads * DK), BF16)] * 2
+        out_shape += [jax.ShapeDtypeStruct((count, tok, key_heads * DK), BF16)] * 2
         scratch.append(pltpu.VMEM((qk_rows.shape[1] + 2 * EDGE, DK), F32))
     else:
-        operands.append(far(mixed))
+        operands.append(mixed)
         in_specs.append(pl.BlockSpec((1, tok, DK), lambda i, lengths: (first + now(i), 0, head)))
     return pl.pallas_call(
         functools.partial(prepare_kernel, first, count, head, group, chunks, key_heads, mixes),
@@ -517,8 +520,8 @@
         cost_estimate=pl.CostEstimate(flops=3 * 10**9 * count, bytes_accessed=4 * 2**20 * count, transcendentals=10**6),
         name="outputs",
     )(
-        lengths, far(qn), far(kn), far(wu), far(starts), far(log_decay), far(write_gain), enter, far(gate_z),
-        far(norm_gain.reshape(1, DV)), far(after if empty else held), far(wu if after is held else after),
+        lengths, qn, kn, wu, starts, far(log_decay), far(write_gain), enter, far(gate_z),
+        far(norm_gain.reshape(1, DV)), far(after if empty else held), far(norm_gain.reshape(1, DV) if after is held else after),
     )
 
 
@@ -742,11 +745,10 @@
 
     for job in jobs:
         mixed = None if job[0] == 0 else made[0][:2]
-        wu, starts, own_map, *new = prepare(
+        wu, starts, own_map, last, *new = prepare(
             job, prompt_lengths, qk_rows, v_in, halo, qk_taps, conv_v, log_decay, write_gain, key_heads,
             mixed and mixed[1], last,
         )
-        last = wu
         moved = [own_map]
         if job == jobs[-1]:
             moved.append(across(own_map, 1))

time: 107 us -> 124 us (1.16)
  local copies, waits for them, and re-layouts: 2.19 us -> 26.6 us
  Pallas kernels: 80.5 us -> 76.1 us
  waiting for transfers between devices: 4.35 us -> 0.86 us
    unnamed x6 -> x34, local copies, waits for them, and re-layouts: 0.66 us -> 25.1 us
    pallas_call x2, Pallas kernels: 50.1 us -> 47.3 us  [prepare(): pl.pallas_call(functools.partial(prepare_kernel, first, count, head, grou...]
    ppermute x1, waiting for transfers between devices: 1.76 us -> 0.01 us  [from_chip_behind(): return lax.ppermute(block, 'seq', route)]
    all_to_all x2, waiting for transfers between devices: 1.74 us -> 0.01 us  [finish(): sent[head] = lax.all_to_all(results[2], 'head', 0, 0)]
    pallas_call x2, Pallas kernels: 23.3 us -> 21.5 us  [outputs(): pl.pallas_call(functools.partial(outputs_kernel, begin, head, group, chun...]
  transfers between devices with their start and end apart: 8 -> 8, of which waited for: 3 -> 1; matrix products, arithmetic and copies ran while one was open for 0% -> 0% of each run, Pallas kernels for 49% -> 40%
where the time goes in v3:
time: 124 us; the launch traced here: 123 us
  Pallas kernels  76.1 us (61%)
  local copies, waits for them, and re-layouts  26.6 us (21%)
  starting transfers between devices  19.1 us (15%)
    pallas_call x2, Pallas kernels, prepare(): pl.pallas_call(functools.partial(prepare_kernel, first, count, head, grou...  47.3 us
    unnamed x34, local copies, waits for them, and re-layouts  25.1 us
    pallas_call x2, Pallas kernels, outputs(): pl.pallas_call(functools.partial(outputs_kernel, begin, head, group, chun...  21.5 us
    all_to_all x2, starting transfers between devices, finish(): sent[head] = lax.all_to_all(results[2], 'head', 0, 0)  11.8 us
    pallas_call x3, Pallas kernels, state_step(): pl.pallas_call(kernel, in_specs=[pl.BlockSpec(memory_space=pltpu.SMEM)] +...  5.84 us
    ppermute x4, starting transfers between devices, across(): return lax.ppermute(block, 'seq', [(i, i ^ distance) for i in range(count)])  4.9 us
  transfers between devices with their start and end apart: 8, of which 1 were waited for; matrix products, arithmetic and copies ran while one was open for 0% of the time, Pallas kernels for 40%

profile of v3, /device:TPU:0, one launch (start us, length us, event | category | flops | bytes accessed | tf_op | source)
XLA Modules:
  0.0 123.4 jit_solution(9636620873726773492)
XLA Ops:
  0.6 0.7 slice.8
  1.4 0.8 slice.7
  2.2 2.4 %collective-permute-start = (bf16[4,32,128]{2,1,0:T(8,128)(2,1)S(1)}, bf16[4,32,128]{2,1,0:T(8,128)(2,1)S(1)}, u32[]{:S(2)}, u32[]{:S(2)}) collective-permute-start(bf16[4,32,128]{2,1,0:T(8,128)(2,1)S(1)} %pad_maximum_fusion), channel_id=1, source_target_pairs={{0,8},{8,16},{16,24},{1,9},{9,17},{17,25},{2,10},{10,18},{18,26},{... | collective-permute-start | bytes 98312 | tf_op jit(solution)/shard_map/ppermute | solution.py:716
  4.6 0.8 collective-permute-done.refs_2_
  5.4 0.0 copy-start.1
  5.4 0.7 copy-done.1
  6.1 24.8 %prepare.2 = (bf16[4,16,256,128]{3,2,1,0:T(8,128)(2,1)S(1)}, bf16[4,2,2048,128]{3,2,1,0:T(8,128)(2,1)S(1)}, bf16[8,256,128]{2,1,0:T(8,128)(2,1)S(1)}, f32[8,128]...) custom-call(s32[4]{0:T(128)S(1)} %copy-done.1, bf16[4,1024,512]{2,1,0:T(8,128)(2,1)} %refs_1_.3, ...), custom_call_target="tpu_custom_call" | custom-call | flops 20000000000 | bytes 16777216 | tf_op jit(solution)/shard_map/prepare/pallas_call | solution.py:397
  30.9 0.0 copy-start.7
  30.9 2.0 %copy-done.7 = bf16[4,16,256,128]{3,2,1,0:T(8,128)(2,1)} copy-done((bf16[4,16,256,128]{3,2,1,0:T(8,128)(2,1)}, bf16[4,16,256,128]{3,2,1,0:T(8,128)(2,1)S(1)}, u32[]{:S(2)}) %copy-start.7) | copy-done | bytes 4194328
  32.9 0.0 copy-start.9
  32.9 2.0 %copy-done.9 = bf16[4,2,2048,128]{3,2,1,0:T(8,128)(2,1)} copy-done((bf16[4,2,2048,128]{3,2,1,0:T(8,128)(2,1)}, bf16[4,2,2048,128]{3,2,1,0:T(8,128)(2,1)S(1)}, u32[]{:S(2)}) %copy-start.9) | copy-done | bytes 4194328
  34.9 0.0 copy-start.11
  34.9 1.3 %copy-done.11 = bf16[4,1024,256]{2,1,0:T(8,128)(2,1)} copy-done((bf16[4,1024,256]{2,1,0:T(8,128)(2,1)}, bf16[4,1024,256]{2,1,0:T(8,128)(2,1)S(1)}, u32[]{:S(2)}) %copy-start.11) | copy-done | bytes 2097176
  36.2 0.0 copy-start.14
  36.2 0.0 collective-permute-start.4
  36.2 4.4 %collective-permute-start.3 = (bf16[8,256,128]{2,1,0:T(8,128)(2,1)S(1)}, bf16[8,256,128]{2,1,0:T(8,128)(2,1)S(1)}, u32[]{:S(2)}, u32[]{:S(2)}) collective-permute-start(bf16[8,256,128]{2,1,0:T(8,128)(2,1)S(1)} %get-tuple-element.26.refs_1_), channel_id=1, source_target_pairs={{0,16},{8,24},{16,0},{24,8},{1,17},{9,25},{17,1},{25,9},{2,18},{10... | collective-permute-start | bytes 1572872 | tf_op jit(solution)/shard_map/ppermute | solution.py:677
  40.6 0.0 collective-permute-start.2
  40.6 0.0 copy-start
  40.6 22.5 %prepare.3 = (bf16[4,16,256,128]{3,2,1,0:T(8,128)(2,1)S(1)}, bf16[4,2,2048,128]{3,2,1,0:T(8,128)(2,1)S(1)}, bf16[8,256,128]{2,1,0:T(8,128)(2,1)S(1)}, f32[8,128]{1,0:T(8,128)}) custom-call(s32[4]{0:T(128)S(1)} %copy-done.1, bf16[4,1024,512]{2,1,0:T(8,128)(2,1)} %refs_1_.3, bf16[4,32,128]{2,1,0:T(8,128)(2,1)S(1)} %collective-permute-done.refs_2_, ...), custom_call_target="tpu_custom_call" | custom-call | flops 20000000000 | bytes 16777216 | tf_op jit(solution)/shard_map/prepare/pallas_call | solution.py:397
  63.1 0.0 copy-done.14
  63.1 0.0 copy-start.3
  63.1 2.0 %copy-done.3 = bf16[4,16,256,128]{3,2,1,0:T(8,128)(2,1)} copy-done((bf16[4,16,256,128]{3,2,1,0:T(8,128)(2,1)}, bf16[4,16,256,128]{3,2,1,0:T(8,128)(2,1)S(1)}, u32[]{:S(2)}) %copy-start.3) | copy-done | bytes 4194328
  65.1 0.0 copy-start.5
  65.1 2.0 %copy-done.5 = bf16[4,2,2048,128]{3,2,1,0:T(8,128)(2,1)} copy-done((bf16[4,2,2048,128]{3,2,1,0:T(8,128)(2,1)}, bf16[4,2,2048,128]{3,2,1,0:T(8,128)(2,1)S(1)}, u32[]{:S(2)}) %copy-start.5) | copy-done | bytes 4194328
  67.1 0.5 collective-permute-start.1
  67.6 0.0 collective-permute-done.4.refs_4_
  67.6 0.0 collective-permute-done.3.refs_3_
  67.6 0.0 collective-permute-done.2.refs_2_
  67.6 0.0 copy-done
  67.6 0.0 copy-start.2
  67.7 2.4 %state_step.3 = (bf16[8,128,128]{2,1,0:T(8,128)(2,1)S(1)}, bf16[8,128,128]{2,1,0:T(8,128)(2,1)}, bf16[8,2,128,128]{3,2,1,0:T(8,128)(2,1)}, f32[8,128]{1,0:T(8,128)}) custom-call(s32[1,8]{1,0:T(1,128)S(1)} %copy-done, bf16[8,256,128]{2,1,0:T(8,128)(2,1)S(1)} %get-tuple-element.26.refs_1_, bf16[8,256,128]{2,1,0:T(8,128)(2,1)S(1)} %collective-permute-done.2.refs_2_, ...), custom_call_target="tpu_custom_call" | custom-call | flops 1000000000 | bytes 1048576 | tf_op jit(solution)/shard_map/state_step/pallas_call | solution.py:644
  70.0 5.8 %all-to-all-start = ((bf16[8,2,128,128]{3,2,1,0:T(8,128)(2,1)}), bf16[8,2,128,128]{3,2,1,0:T(8,128)(2,1)S(1)}, u32[]{:S(2)}, u32[]{:S(2)}) async-start(bf16[8,2,128,128]{3,2,1,0:T(8,128)(2,1)} %get-tuple-element.36), calls=%async_computation | async-start | bytes 1048576 | tf_op jit(solution)/shard_map/all_to_all | solution.py:732
  75.9 0.0 collective-permute-done.1.refs_2_
  75.9 1.4 %state_step.4 = (bf16[8,256,128]{2,1,0:T(8,128)(2,1)S(1)}, f32[8,128]{1,0:T(8,128)}) custom-call(s32[1,8]{1,0:T(1,128)S(1)} %copy-done, bf16[8,256,128]{2,1,0:T(8,128)(2,1)S(1)} %get-tuple-element.25.refs_1_, bf16[8,256,128]{2,1,0:T(8,128)(2,1)S(1)} %collective-permute-done.1.refs_2_, f32[8,128]{1,0:T(8,128)} %get-tuple-element.28.refs_3_), custom_call_target="tpu_custom_call" | custom-call | flops 1000000000 | bytes 1048576 | tf_op jit(solution)/shard_map/state_step/pallas_call | solution.py:644
  77.2 0.0 collective-permute-start.5
  77.2 0.0 copy-done.2
  77.2 0.0 copy-start.8
  77.2 2.2 %copy-done.8 = bf16[4,16,256,128]{3,2,1,0:T(8,128)(2,1)S(1)} copy-done((bf16[4,16,256,128]{3,2,1,0:T(8,128)(2,1)S(1)}, bf16[4,16,256,128]{3,2,1,0:T(8,128)(2,1)}, u32[]{:S(2)}) %copy-start.8) | copy-done | bytes 4194328
  79.4 0.0 copy-start.10
  79.4 2.2 %copy-done.10 = bf16[4,2,2048,128]{3,2,1,0:T(8,128)(2,1)S(1)} copy-done((bf16[4,2,2048,128]{3,2,1,0:T(8,128)(2,1)S(1)}, bf16[4,2,2048,128]{3,2,1,0:T(8,128)(2,1)}, u32[]{:S(2)}) %copy-start.10) | copy-done | bytes 4194328
  81.6 0.0 copy-start.12
  81.6 1.6 %copy-done.12 = bf16[4,1024,256]{2,1,0:T(8,128)(2,1)S(1)} copy-done((bf16[4,1024,256]{2,1,0:T(8,128)(2,1)S(1)}, bf16[4,1024,256]{2,1,0:T(8,128)(2,1)}, u32[]{:S(2)}) %copy-start.12) | copy-done | bytes 2097176
  83.2 0.0 copy-start.15
  83.2 1.6 %copy-done.15 = bf16[4,1024,256]{2,1,0:T(8,128)(2,1)S(1)} copy-done((bf16[4,1024,256]{2,1,0:T(8,128)(2,1)S(1)}, bf16[4,1024,256]{2,1,0:T(8,128)(2,1)}, u32[]{:S(2)}) %copy-start.15) | copy-done | bytes 2097176
  84.8 10.7 %outputs.2.refs_5_.held_ref = bf16[4,1024,512]{2,1,0:T(8,128)(2,1)} custom-call(s32[4]{0:T(128)S(1)} %copy-done.2, bf16[4,1024,256]{2,1,0:T(8,128)(2,1)S(1)} %copy-done.12, bf16[4,1024,256]{2,1,0:T(8,128)(2,1)S(1)} %copy-done.15, bf16[4,16,256,128]{3,2,1,0:T(8,128)(2,1)S(1)} %copy-done.8, bf16[4,2,2048,128]{3,2,1,0:T(8,128)(2,1)S(1)} %copy-done.10, ...), custom_call_target="tpu_custom_call" | custom-call | flops 12000000000 | bytes 16777216 | tf_op jit(solution)/shard_map/outputs/pallas_call | solution.py:492
  95.5 0.0 collective-permute-done.5.refs_4_
  95.5 2.1 %state_step.5 = (bf16[8,128,128]{2,1,0:T(8,128)(2,1)S(1)}, bf16[8,128,128]{2,1,0:T(8,128)(2,1)}, bf16[8,2,128,128]{3,2,1,0:T(8,128)(2,1)}, f32[8,128]{1,0:T(8,128)}) custom-call(s32[1,8]{1,0:T(1,128)S(1)} %copy-done, bf16[8,256,128]{2,1,0:T(8,128)(2,1)S(1)} %get-tuple-element.25.refs_1_, bf16[8,256,128]{2,1,0:T(8,128)(2,1)S(1)} %collective-permute-done.1.refs_2_, ...), custom_call_target="tpu_custom_call" | custom-call | flops 1000000000 | bytes 1048576 | tf_op jit(solution)/shard_map/state_step/pallas_call | solution.py:644
  97.6 0.0 all-to-all-done.refs_0_
  97.6 6.0 %all-to-all-start.1 = ((bf16[8,2,128,128]{3,2,1,0:T(8,128)(2,1)}), bf16[8,2,128,128]{3,2,1,0:T(8,128)(2,1)S(1)}, u32[]{:S(2)}, u32[]{:S(2)}) async-start(bf16[8,2,128,128]{3,2,1,0:T(8,128)(2,1)} %get-tuple-element.37), calls=%async_computation.1 | async-start | bytes 1048576 | tf_op jit(solution)/shard_map/all_to_all | solution.py:732
  103.7 0.0 copy-start.4
  103.7 2.2 %copy-done.4 = bf16[4,16,256,128]{3,2,1,0:T(8,128)(2,1)S(1)} copy-done((bf16[4,16,256,128]{3,2,1,0:T(8,128)(2,1)S(1)}, bf16[4,16,256,128]{3,2,1,0:T(8,128)(2,1)}, u32[]{:S(2)}) %copy-start.4) | copy-done | bytes 4194328
  105.9 0.0 copy-start.6
  105.9 2.2 %copy-done.6 = bf16[4,2,2048,128]{3,2,1,0:T(8,128)(2,1)S(1)} copy-done((bf16[4,2,2048,128]{3,2,1,0:T(8,128)(2,1)S(1)}, bf16[4,2,2048,128]{3,2,1,0:T(8,128)(2,1)}, u32[]{:S(2)}) %copy-start.6) | copy-done | bytes 4194328
  108.0 0.0 copy-start.13
  108.0 1.6 %copy-done.13 = bf16[4,1024,256]{2,1,0:T(8,128)(2,1)S(1)} copy-done((bf16[4,1024,256]{2,1,0:T(8,128)(2,1)S(1)}, bf16[4,1024,256]{2,1,0:T(8,128)(2,1)}, u32[]{:S(2)}) %copy-start.13) | copy-done | bytes 2097176
  109.6 0.0 copy-start.16
  109.6 1.6 %copy-done.16 = bf16[4,1024,256]{2,1,0:T(8,128)(2,1)S(1)} copy-done((bf16[4,1024,256]{2,1,0:T(8,128)(2,1)S(1)}, bf16[4,1024,256]{2,1,0:T(8,128)(2,1)}, u32[]{:S(2)}) %copy-start.16) | copy-done | bytes 2097176
  111.2 10.8 %outputs.3 = bf16[4,1024,512]{2,1,0:T(8,128)(2,1)} custom-call(s32[4]{0:T(128)S(1)} %copy-done.2, bf16[4,1024,256]{2,1,0:T(8,128)(2,1)S(1)} %copy-done.13, bf16[4,1024,256]{2,1,0:T(8,128)(2,1)S(1)} %copy-done.16, bf16[4,16,256,128]{3,2,1,0:T(8,128)(2,1)S(1)} %copy-done.4, bf16[4,2,2048,128]{3,2,1,0:T(8,128)(2,1)S(1)} %copy-done.6, ...), custom_call_target="tpu_custom_call", output_to_operand_aliasing={{}: (10, {})} | custom-call | flops 12000000000 | bytes 16777216 | tf_op jit(solution)/shard_map/outputs/pallas_call | solution.py:492
  122.0 0.0 all-to-all-done.1.refs_1_
  122.0 1.4 %deliver.1 = f32[8,4,128,128]{3,2,1,0:T(8,128)} custom-call(bf16[8,2,128,128]{3,2,1,0:T(8,128)(2,1)S(1)} %all-to-all-done.refs_0_, bf16[8,2,128,128]{3,2,1,0:T(8,128)(2,1)S(1)} %all-to-all-done.1.refs_1_), custom_call_target="tpu_custom_call" | custom-call | tf_op jit(solution)/shard_map/deliver/pallas_call | solution.py:664
  (3 shorter events, 0.0 us)
Async XLA Ops:
  2.2 3.2 %collective-permute-start = (bf16[4,32,128]{2,1,0:T(8,128)(2,1)S(1)}, bf16[4,32,128]{2,1,0:T(8,128)(2,1)S(1)}, u32[]{:S(2)}, u32[]{:S(2)}) collective-permute-start(bf16[4,32,128]{2,1,0:T(8,128)(2,1)S(1)} %pad_maximum_fusion), channel_id=1, source_target_pairs={{0,8},{8,16},{16,24},{1,9},{9,17},{17,25},{2,10},{10,18},{18,26},{... | collective-permute-start | bytes 98312 | tf_op jit(solution)/shard_map/ppermute | solution.py:716
  5.4 0.7 copy-start.1
  30.9 2.0 %copy-start.7 = (bf16[4,16,256,128]{3,2,1,0:T(8,128)(2,1)}, bf16[4,16,256,128]{3,2,1,0:T(8,128)(2,1)S(1)}, u32[]{:S(2)}) copy-start(bf16[4,16,256,128]{3,2,1,0:T(8,128)(2,1)S(1)} %get-tuple-element.30.wu_ref) | copy-start | bytes 12582916
  32.9 2.0 %copy-start.9 = (bf16[4,2,2048,128]{3,2,1,0:T(8,128)(2,1)}, bf16[4,2,2048,128]{3,2,1,0:T(8,128)(2,1)S(1)}, u32[]{:S(2)}) copy-start(bf16[4,2,2048,128]{3,2,1,0:T(8,128)(2,1)S(1)} %get-tuple-element.31.start_ref) | copy-start | bytes 12582916
  34.9 1.3 %copy-start.11 = (bf16[4,1024,256]{2,1,0:T(8,128)(2,1)}, bf16[4,1024,256]{2,1,0:T(8,128)(2,1)S(1)}, u32[]{:S(2)}) copy-start(bf16[4,1024,256]{2,1,0:T(8,128)(2,1)S(1)} %get-tuple-element.20.qn_ref) | copy-start | bytes 6291460
  36.2 26.9 %copy-start.14 = (bf16[4,1024,256]{2,1,0:T(8,128)(2,1)}, bf16[4,1024,256]{2,1,0:T(8,128)(2,1)S(1)}, u32[]{:S(2)}) copy-start(bf16[4,1024,256]{2,1,0:T(8,128)(2,1)S(1)} %get-tuple-element.21.refs_7_.kn_ref) | copy-start | bytes 6291460
  36.2 31.4 %collective-permute-start.4 = (bf16[8,256,128]{2,1,0:T(8,128)(2,1)S(1)}, bf16[8,256,128]{2,1,0:T(8,128)(2,1)S(1)}, u32[]{:S(2)}, u32[]{:S(2)}) collective-permute-start(bf16[8,256,128]{2,1,0:T(8,128)(2,1)S(1)} %get-tuple-element.26.refs_1_), channel_id=1, source_target_pairs={{0,24},{8,16},{16,8},{24,0},{1,25},{9,17},{17,9},{25,1},{2,26},{10... | collective-permute-start | bytes 1572872 | tf_op jit(solution)/shard_map/ppermute | solution.py:677
  36.2 31.4 %collective-permute-start.3 = (bf16[8,256,128]{2,1,0:T(8,128)(2,1)S(1)}, bf16[8,256,128]{2,1,0:T(8,128)(2,1)S(1)}, u32[]{:S(2)}, u32[]{:S(2)}) collective-permute-start(bf16[8,256,128]{2,1,0:T(8,128)(2,1)S(1)} %get-tuple-element.26.refs_1_), channel_id=1, source_target_pairs={{0,16},{8,24},{16,0},{24,8},{1,17},{9,25},{17,1},{25,9},{2,18},{10... | collective-permute-start | bytes 1572872 | tf_op jit(solution)/shard_map/ppermute | solution.py:677
  40.6 27.0 %collective-permute-start.2 = (bf16[8,256,128]{2,1,0:T(8,128)(2,1)S(1)}, bf16[8,256,128]{2,1,0:T(8,128)(2,1)S(1)}, u32[]{:S(2)}, u32[]{:S(2)}) collective-permute-start(bf16[8,256,128]{2,1,0:T(8,128)(2,1)S(1)} %get-tuple-element.26.refs_1_), channel_id=1, source_target_pairs={{0,8},{8,0},{16,24},{24,16},{1,9},{9,1},{17,25},{25,17},{2,10},{10... | collective-permute-start | bytes 1572872 | tf_op jit(solution)/shard_map/ppermute | solution.py:677
  40.6 27.0 %copy-start = (s32[1,8]{1,0:T(1,128)S(1)}, s32[1,8]{1,0:T(1,128)}, u32[]{:S(2)}) copy-start(s32[1,8]{1,0:T(1,128)} %refs_0_.9) | copy-start | bytes 100
  63.1 2.0 %copy-start.3 = (bf16[4,16,256,128]{3,2,1,0:T(8,128)(2,1)}, bf16[4,16,256,128]{3,2,1,0:T(8,128)(2,1)S(1)}, u32[]{:S(2)}) copy-start(bf16[4,16,256,128]{3,2,1,0:T(8,128)(2,1)S(1)} %get-tuple-element.23.wu_ref) | copy-start | bytes 12582916
  65.1 2.0 %copy-start.5 = (bf16[4,2,2048,128]{3,2,1,0:T(8,128)(2,1)}, bf16[4,2,2048,128]{3,2,1,0:T(8,128)(2,1)S(1)}, u32[]{:S(2)}) copy-start(bf16[4,2,2048,128]{3,2,1,0:T(8,128)(2,1)S(1)} %get-tuple-element.24.start_ref) | copy-start | bytes 12582916
  67.1 8.7 %collective-permute-start.1 = (bf16[8,256,128]{2,1,0:T(8,128)(2,1)S(1)}, bf16[8,256,128]{2,1,0:T(8,128)(2,1)S(1)}, u32[]{:S(2)}, u32[]{:S(2)}) collective-permute-start(bf16[8,256,128]{2,1,0:T(8,128)(2,1)S(1)} %get-tuple-element.25.refs_1_), channel_id=1, source_target_pairs={{0,8},{8,0},{16,24},{24,16},{1,9},{9,1},{17,25},{25,17},{2,10},{10... | collective-permute-start | bytes 1572872 | tf_op jit(solution)/shard_map/ppermute | solution.py:677
  67.6 9.6 %copy-start.2 = (s32[4]{0:T(128)S(1)}, s32[4]{0:T(128)}, u32[]{:S(2)}) copy-start(s32[4]{0:T(128)} %length_ref.3) | copy-start | bytes 52
  70.0 27.6 %all-to-all-start = ((bf16[8,2,128,128]{3,2,1,0:T(8,128)(2,1)}), bf16[8,2,128,128]{3,2,1,0:T(8,128)(2,1)S(1)}, u32[]{:S(2)}, u32[]{:S(2)}) async-start(bf16[8,2,128,128]{3,2,1,0:T(8,128)(2,1)} %get-tuple-element.36), calls=%async_computation | async-start | bytes 1048576 | tf_op jit(solution)/shard_map/all_to_all | solution.py:732
  77.2 18.3 %collective-permute-start.5 = (bf16[8,256,128]{2,1,0:T(8,128)(2,1)S(1)}, bf16[8,256,128]{2,1,0:T(8,128)(2,1)S(1)}, u32[]{:S(2)}, u32[]{:S(2)}) collective-permute-start(bf16[8,256,128]{2,1,0:T(8,128)(2,1)S(1)} %get-tuple-element.29.refs_3_), channel_id=1, source_target_pairs={{0,16},{8,24},{16,0},{24,8},{1,17},{9,25},{17,1},{25,9},{2,18},{10... | collective-permute-start | bytes 1572872 | tf_op jit(solution)/shard_map/ppermute | solution.py:684
  77.2 2.2 %copy-start.8 = (bf16[4,16,256,128]{3,2,1,0:T(8,128)(2,1)S(1)}, bf16[4,16,256,128]{3,2,1,0:T(8,128)(2,1)}, u32[]{:S(2)}) copy-start(bf16[4,16,256,128]{3,2,1,0:T(8,128)(2,1)} %copy-done.7) | copy-start | bytes 12582916
  79.4 2.2 %copy-start.10 = (bf16[4,2,2048,128]{3,2,1,0:T(8,128)(2,1)S(1)}, bf16[4,2,2048,128]{3,2,1,0:T(8,128)(2,1)}, u32[]{:S(2)}) copy-start(bf16[4,2,2048,128]{3,2,1,0:T(8,128)(2,1)} %copy-done.9) | copy-start | bytes 12582916
  81.6 1.6 %copy-start.12 = (bf16[4,1024,256]{2,1,0:T(8,128)(2,1)S(1)}, bf16[4,1024,256]{2,1,0:T(8,128)(2,1)}, u32[]{:S(2)}) copy-start(bf16[4,1024,256]{2,1,0:T(8,128)(2,1)} %copy-done.11) | copy-start | bytes 6291460
  83.2 1.6 %copy-start.15 = (bf16[4,1024,256]{2,1,0:T(8,128)(2,1)S(1)}, bf16[4,1024,256]{2,1,0:T(8,128)(2,1)}, u32[]{:S(2)}) copy-start(bf16[4,1024,256]{2,1,0:T(8,128)(2,1)} %copy-done.14) | copy-start | bytes 6291460
  97.6 24.4 %all-to-all-start.1 = ((bf16[8,2,128,128]{3,2,1,0:T(8,128)(2,1)}), bf16[8,2,128,128]{3,2,1,0:T(8,128)(2,1)S(1)}, u32[]{:S(2)}, u32[]{:S(2)}) async-start(bf16[8,2,128,128]{3,2,1,0:T(8,128)(2,1)} %get-tuple-element.37), calls=%async_computation.1 | async-start | bytes 1048576 | tf_op jit(solution)/shard_map/all_to_all | solution.py:732
  103.7 2.2 %copy-start.4 = (bf16[4,16,256,128]{3,2,1,0:T(8,128)(2,1)S(1)}, bf16[4,16,256,128]{3,2,1,0:T(8,128)(2,1)}, u32[]{:S(2)}) copy-start(bf16[4,16,256,128]{3,2,1,0:T(8,128)(2,1)} %copy-done.3) | copy-start | bytes 12582916
  105.9 2.2 %copy-start.6 = (bf16[4,2,2048,128]{3,2,1,0:T(8,128)(2,1)S(1)}, bf16[4,2,2048,128]{3,2,1,0:T(8,128)(2,1)}, u32[]{:S(2)}) copy-start(bf16[4,2,2048,128]{3,2,1,0:T(8,128)(2,1)} %copy-done.5) | copy-start | bytes 12582916
  108.0 1.6 %copy-start.13 = (bf16[4,1024,256]{2,1,0:T(8,128)(2,1)S(1)}, bf16[4,1024,256]{2,1,0:T(8,128)(2,1)}, u32[]{:S(2)}) copy-start(bf16[4,1024,256]{2,1,0:T(8,128)(2,1)} %copy-done.11) | copy-start | bytes 6291460
  109.6 1.6 %copy-start.16 = (bf16[4,1024,256]{2,1,0:T(8,128)(2,1)S(1)}, bf16[4,1024,256]{2,1,0:T(8,128)(2,1)}, u32[]{:S(2)}) copy-start(bf16[4,1024,256]{2,1,0:T(8,128)(2,1)} %copy-done.14) | copy-start | bytes 6291460

commit v4 on v3

--- a/solution.py
+++ b/solution.py
@@ -14,7 +14,7 @@
 TINY = 16
 EDGE = 8
 EPSILON = 1e-06
-VMEM_BYTES = 24 * 1024 * 1024
+VMEM_BYTES = 40 * 1024 * 1024
 SMALL_VMEM_BYTES = 8 * 1024 * 1024
 F32 = jnp.float32
 BF16 = jnp.bfloat16
@@ -199,15 +199,16 @@
         if mixes:
             mix(qk_ref, halo_ref, qk_taps_ref, qn_ref, kn_ref, raw_scr, key_heads, chunks)
         halo = halo_ref[0].astype(F32)
-        v_pad[EDGE:, :] = v_ref[0].astype(F32)
+        for h in range(group):
+            columns = slice(h * DV, (h + 1) * DV)
+            v_pad[pl.ds(EDGE + h, chunks * BLOCK, group), :] = v_ref[0, :, columns].astype(F32)
         for i in range(CONV - 1):
             for h in range(group):
                 source = 2 * EDGE + (i * key_heads + head) * group + h
-                v_pad[EDGE - CONV + 1 + i : EDGE - CONV + 2 + i, h * DV : (h + 1) * DV] = halo[
-                    source : source + 1
-                ]
+                to = EDGE + (i - CONV + 1) * group + h
+                v_pad[to : to + 1, :] = halo[source : source + 1]
         v_all_taps = v_taps_ref[...].astype(F32)
-        v_taps = [v_all_taps[i : i + 1] for i in range(CONV)]
+        v_taps = [[v_all_taps[i : i + 1, h * DV : (h + 1) * DV] for i in range(CONV)] for h in range(group)]
 
         cum, gain = gates_of_heads(log_ref, gain_ref, used, head, group)
         both_gains = gain * jnp.exp(cum)
@@ -228,7 +229,7 @@
         turned = {}
 
         def front(some):
-            ops, kk, later, compact, solved, mixed = [], {}, {}, {}, {}, {}
+            ops, kk, later, compact, solved = [], {}, {}, {}, {}
             local = [(h, c) for c in some for h in range(group)]
 
             def start(c):
@@ -254,12 +255,9 @@
                 for b in range(BLOCK // TINY):
                     x_scr[r, b * TINY : (b + 1) * TINY, :] = jnp.where(part_of == b, solved[r], 0.0).astype(BF16)
 
-            def convolve(c):
-                mixed[c] = mixed_rows(v_pad, v_taps, EDGE, 0, 1, c).astype(BF16)
-
             def scale(h, c):
                 top = h * (DK + DV)
-                v_wide = mixed[c][:, h * DV : (h + 1) * DV].T.astype(F32)
+                v_wide = mixed_rows(v_pad, v_taps[h], EDGE, h, group, c).astype(BF16).T.astype(F32)
                 y_scr[c, top : top + DK, :] = (turned[c].astype(F32) * both_gains[h : h + 1, span(c)]).astype(BF16)
                 y_scr[c, top + DK : top + DK + DV, :] = (v_wide * gain[h : h + 1, span(c)]).astype(BF16)
 
@@ -274,7 +272,6 @@
                 ops.append(functools.partial(place, h * chunks + c))
             right = []
             for c in some:
-                right.append(functools.partial(convolve, c))
                 right += [functools.partial(scale, h, c) for h in range(group)]
             return ops, right
 
@@ -367,13 +364,13 @@
         pl.BlockSpec((8, 128), lambda i, lengths: (0, 0)),
     ]
     out_shape = [
-        jax.ShapeDtypeStruct((count, rows, DK + DV, BLOCK), BF16),
-        jax.ShapeDtypeStruct((count, group, chunks * (DV + DK), DK), BF16),
+        pltpu.HBM((count, rows, DK + DV, BLOCK), BF16),
+        pltpu.HBM((count, group, chunks * (DV + DK), DK), BF16),
         jax.ShapeDtypeStruct((count * group, DV + DK, DK), BF16),
         pltpu.HBM((8, 128), F32),
     ]
     scratch = [
-        pltpu.VMEM((tok + EDGE, wide), F32),
+        pltpu.VMEM((tok * group + EDGE, DV), F32),
         pltpu.VMEM((2, chunks, group, DK, DK), BF16),
         pltpu.VMEM((2, chunks, group, DV, DK), F32),
         pltpu.VMEM((2, chunks, group, BLOCK), F32),
@@ -389,10 +386,10 @@
             pl.BlockSpec(qk_taps.shape, lambda i, lengths: (0, 0)),
         ]
         out_specs += [pl.BlockSpec((1, tok, key_heads * DK), lambda i, lengths: (now(i), 0, 0))] * 2
-        out_shape += [jax.ShapeDtypeStruct((count, tok, key_heads * DK), BF16)] * 2
+        out_shape += [pltpu.HBM((count, tok, key_heads * DK), BF16)] * 2
         scratch.append(pltpu.VMEM((qk_rows.shape[1] + 2 * EDGE, DK), F32))
     else:
-        operands.append(mixed)
+        operands.append(far(mixed))
         in_specs.append(pl.BlockSpec((1, tok, DK), lambda i, lengths: (first + now(i), 0, head)))
     return pl.pallas_call(
         functools.partial(prepare_kernel, first, count, head, group, chunks, key_heads, mixes),
@@ -407,7 +404,7 @@
         compiler_params=pltpu.CompilerParams(vmem_limit_bytes=VMEM_BYTES),
         cost_estimate=pl.CostEstimate(flops=5 * 10**9 * count, bytes_accessed=4 * 2**20 * count, transcendentals=10**6),
         name="prepare",
-    )(lengths, *operands)
+    )(far(lengths), *operands)
 
 
 def outputs_kernel(
@@ -520,7 +517,7 @@
         cost_estimate=pl.CostEstimate(flops=3 * 10**9 * count, bytes_accessed=4 * 2**20 * count, transcendentals=10**6),
         name="outputs",
     )(
-        lengths, qn, kn, wu, starts, far(log_decay), far(write_gain), enter, far(gate_z),
+        far(lengths), far(qn), far(kn), far(wu), far(starts), far(log_decay), far(write_gain), enter, far(gate_z),
         far(norm_gain.reshape(1, DV)), far(after if empty else held), far(norm_gain.reshape(1, DV) if after is held else after),
     )
 

time: 124 us -> 104 us (0.84)
  local copies, waits for them, and re-layouts: 26.6 us -> 1.53 us
  waiting for transfers between devices: 0.86 us -> 4.12 us
  Pallas kernels: 76.1 us -> 77.9 us
    unnamed x34 -> x2, local copies, waits for them, and re-layouts: 25.1 us -> 0.01 us
    pallas_call x2, Pallas kernels: 21.5 us -> 23.5 us  [outputs(): pl.pallas_call(functools.partial(outputs_kernel, begin, head, group, chun...]
    ppermute x1, waiting for transfers between devices: 0.01 us -> 1.64 us  [from_chip_behind(): return lax.ppermute(block, 'seq', route)]
    all_to_all x2, waiting for transfers between devices: 0.01 us -> 1.63 us  [finish(): sent[head] = lax.all_to_all(results[2], 'head', 0, 0)]
  transfers between devices with their start and end apart: 8 -> 8, of which waited for: 1 -> 3; matrix products, arithmetic and copies ran while one was open for 0% -> 0% of each run, Pallas kernels for 40% -> 50%
where the time goes in v4:
time: 104 us; the launch traced here: 103 us
  Pallas kernels  77.9 us (75%)
  starting transfers between devices  18.8 us (18%)
  waiting for transfers between devices  4.12 us (4%)
  local copies, waits for them, and re-layouts  1.53 us (1%)
    pallas_call x2, Pallas kernels, prepare(): pl.pallas_call(functools.partial(prepare_kernel, first, count, head, grou...  47.4 us
    pallas_call x2, Pallas kernels, outputs(): pl.pallas_call(functools.partial(outputs_kernel, begin, head, group, chun...  23.5 us
    all_to_all x2, starting transfers between devices, finish(): sent[head] = lax.all_to_all(results[2], 'head', 0, 0)  11.5 us
    pallas_call x3, Pallas kernels, state_step(): pl.pallas_call(kernel, in_specs=[pl.BlockSpec(memory_space=pltpu.SMEM)] +...  5.61 us
    ppermute x4, starting transfers between devices, across(): return lax.ppermute(block, 'seq', [(i, i ^ distance) for i in range(count)])  4.92 us
    ppermute x1, starting transfers between devices, shards(): lax.ppermute(tails, 'seq', [(i, i + 1) for i in range(seq_count - 1)])  2.36 us
  transfers between devices with their start and end apart: 8, of which 3 were waited for; matrix products, arithmetic and copies ran while one was open for 0% of the time, Pallas kernels for 50%

profile of v4, /device:TPU:0, one launch (start us, length us, event | category | flops | bytes accessed | tf_op | source)
XLA Modules:
  0.0 103.1 jit_solution(2748834602294574242)
XLA Ops:
  0.6 0.7 slice.8
  1.4 0.8 slice.7
  2.2 2.4 %collective-permute-start = (bf16[4,32,128]{2,1,0:T(8,128)(2,1)S(1)}, bf16[4,32,128]{2,1,0:T(8,128)(2,1)S(1)}, u32[]{:S(2)}, u32[]{:S(2)}) collective-permute-start(bf16[4,32,128]{2,1,0:T(8,128)(2,1)S(1)} %pad_maximum_fusion), channel_id=1, source_target_pairs={{0,8},{8,16},{16,24},{1,9},{9,17},{17,25},{2,10},{10,18},{18,26},{... | collective-permute-start | bytes 98312 | tf_op jit(solution)/shard_map/ppermute | solution.py:713
  4.6 0.8 collective-permute-done.refs_2_
  5.4 24.8 %prepare.2 = (bf16[4,16,256,128]{3,2,1,0:T(8,128)(2,1)}, bf16[4,2,2048,128]{3,2,1,0:T(8,128)(2,1)}, bf16[8,256,128]{2,1,0:T(8,128)(2,1)S(1)}, f32[8,128]{1,0:T(8...) custom-call(s32[4]{0:T(128)} %length_ref.3, bf16[4,1024,512]{2,1,0:T(8,128)(2,1)} %refs_1_.3, ...), custom_call_target="tpu_custom_call" | custom-call | flops 20000000000 | bytes 16777216 | tf_op jit(solution)/shard_map/prepare/pallas_call | solution.py:394
  30.2 0.0 collective-permute-start.4
  30.3 4.4 %collective-permute-start.3 = (bf16[8,256,128]{2,1,0:T(8,128)(2,1)S(1)}, bf16[8,256,128]{2,1,0:T(8,128)(2,1)S(1)}, u32[]{:S(2)}, u32[]{:S(2)}) collective-permute-start(bf16[8,256,128]{2,1,0:T(8,128)(2,1)S(1)} %get-tuple-element.26.refs_1_), channel_id=1, source_target_pairs={{0,16},{8,24},{16,0},{24,8},{1,17},{9,25},{17,1},{25,9},{2,18},{10... | collective-permute-start | bytes 1572872 | tf_op jit(solution)/shard_map/ppermute | solution.py:674
  34.7 0.0 collective-permute-start.2
  34.7 0.0 copy-start
  34.7 22.5 %prepare.3 = (bf16[4,16,256,128]{3,2,1,0:T(8,128)(2,1)}, bf16[4,2,2048,128]{3,2,1,0:T(8,128)(2,1)}, bf16[8,256,128]{2,1,0:T(8,128)(2,1)S(1)}, f32[8,128]{1,0:T(8,128)}) custom-call(s32[4]{0:T(128)} %length_ref.3, bf16[4,1024,512]{2,1,0:T(8,128)(2,1)} %refs_1_.3, bf16[4,32,128]{2,1,0:T(8,128)(2,1)S(1)} %collective-permute-done.refs_2_, ...), custom_call_target="tpu_custom_call" | custom-call | flops 20000000000 | bytes 16777216 | tf_op jit(solution)/shard_map/prepare/pallas_call | solution.py:394
  57.2 0.5 collective-permute-start.1
  57.7 0.0 collective-permute-done.4.refs_4_
  57.7 0.0 collective-permute-done.3.refs_3_
  57.7 0.0 collective-permute-done.2.refs_2_
  57.7 0.0 copy-done
  57.7 2.2 %state_step.3 = (bf16[8,128,128]{2,1,0:T(8,128)(2,1)S(1)}, bf16[8,128,128]{2,1,0:T(8,128)(2,1)}, bf16[8,2,128,128]{3,2,1,0:T(8,128)(2,1)}, f32[8,128]{1,0:T(8,128)}) custom-call(s32[1,8]{1,0:T(1,128)S(1)} %copy-done, bf16[8,256,128]{2,1,0:T(8,128)(2,1)S(1)} %get-tuple-element.26.refs_1_, bf16[8,256,128]{2,1,0:T(8,128)(2,1)S(1)} %collective-permute-done.2.refs_2_, ...), custom_call_target="tpu_custom_call" | custom-call | flops 1000000000 | bytes 1048576 | tf_op jit(solution)/shard_map/state_step/pallas_call | solution.py:641
  59.9 5.8 %all-to-all-start = ((bf16[8,2,128,128]{3,2,1,0:T(8,128)(2,1)}), bf16[8,2,128,128]{3,2,1,0:T(8,128)(2,1)S(1)}, u32[]{:S(2)}, u32[]{:S(2)}) async-start(bf16[8,2,128,128]{3,2,1,0:T(8,128)(2,1)} %get-tuple-element.36), calls=%async_computation | async-start | bytes 1048576 | tf_op jit(solution)/shard_map/all_to_all | solution.py:729
  65.7 0.0 collective-permute-done.1.refs_2_
  65.7 1.4 %state_step.4 = (bf16[8,256,128]{2,1,0:T(8,128)(2,1)S(1)}, f32[8,128]{1,0:T(8,128)}) custom-call(s32[1,8]{1,0:T(1,128)S(1)} %copy-done, bf16[8,256,128]{2,1,0:T(8,128)(2,1)S(1)} %get-tuple-element.25.refs_1_, bf16[8,256,128]{2,1,0:T(8,128)(2,1)S(1)} %collective-permute-done.1.refs_2_, f32[8,128]{1,0:T(8,128)} %get-tuple-element.28.refs_3_), custom_call_target="tpu_custom_call" | custom-call | flops 1000000000 | bytes 1048576 | tf_op jit(solution)/shard_map/state_step/pallas_call | solution.py:641
  67.1 0.0 collective-permute-start.5
  67.1 11.9 %outputs.2.refs_5_.held_ref = bf16[4,1024,512]{2,1,0:T(8,128)(2,1)} custom-call(s32[4]{0:T(128)} %length_ref.3, bf16[4,1024,256]{2,1,0:T(8,128)(2,1)} %get-tuple-element.20.qn_ref, bf16[4,1024,256]{2,1,0:T(8,128)(2,1)} %get-tuple-element.21.refs_7_.kn_ref, bf16[4,16,256,128]{3,2,1,0:T(8,128)(2,1)} %get-tuple-element.30.wu_ref, ...), custom_call_target="tpu_custom_call" | custom-call | flops 12000000000 | bytes 16777216 | tf_op jit(solution)/shard_map/outputs/pallas_call | solution.py:489
  79.1 1.6 %collective-permute-done.5.refs_4_ = bf16[8,256,128]{2,1,0:T(8,128)(2,1)S(1)} collective-permute-done((bf16[8,256,128]{2,1,0:T(8,128)(2,1)S(1)}, bf16[8,256,128]{2,1,0:T(8,128)(2,1)S(1)}, u32[]{:S(2)}, u32[]{:S(2)}) %collective-permute-start.5) | collective-permute-done | bytes 524320 | tf_op jit(solution)/shard_map/ppermute | solution.py:681
  80.7 2.1 %state_step.5 = (bf16[8,128,128]{2,1,0:T(8,128)(2,1)S(1)}, bf16[8,128,128]{2,1,0:T(8,128)(2,1)}, bf16[8,2,128,128]{3,2,1,0:T(8,128)(2,1)}, f32[8,128]{1,0:T(8,128)}) custom-call(s32[1,8]{1,0:T(1,128)S(1)} %copy-done, bf16[8,256,128]{2,1,0:T(8,128)(2,1)S(1)} %get-tuple-element.25.refs_1_, bf16[8,256,128]{2,1,0:T(8,128)(2,1)S(1)} %collective-permute-done.1.refs_2_, ...), custom_call_target="tpu_custom_call" | custom-call | flops 1000000000 | bytes 1048576 | tf_op jit(solution)/shard_map/state_step/pallas_call | solution.py:641
  82.8 0.0 all-to-all-done.refs_0_
  82.8 5.7 %all-to-all-start.1 = ((bf16[8,2,128,128]{3,2,1,0:T(8,128)(2,1)}), bf16[8,2,128,128]{3,2,1,0:T(8,128)(2,1)S(1)}, u32[]{:S(2)}, u32[]{:S(2)}) async-start(bf16[8,2,128,128]{3,2,1,0:T(8,128)(2,1)} %get-tuple-element.37), calls=%async_computation.1 | async-start | bytes 1048576 | tf_op jit(solution)/shard_map/all_to_all | solution.py:729
  88.5 11.6 %outputs.3 = bf16[4,1024,512]{2,1,0:T(8,128)(2,1)} custom-call(s32[4]{0:T(128)} %length_ref.3, bf16[4,1024,256]{2,1,0:T(8,128)(2,1)} %get-tuple-element.20.qn_ref, bf16[4,1024,256]{2,1,0:T(8,128)(2,1)} %get-tuple-element.21.refs_7_.kn_ref, bf16[4,16,256,128]{3,2,1,0:T(8,128)(2,1)} %get-tuple-element.23.wu_ref, ...), custom_call_target="tpu_custom_call", output_to_operand_aliasing={{}: (10, {})} | custom-call | flops 12000000000 | bytes 16777216 | tf_op jit(solution)/shard_map/outputs/pallas_call | solution.py:489
  100.1 1.6 %all-to-all-done.1.refs_1_ = bf16[8,2,128,128]{3,2,1,0:T(8,128)(2,1)S(1)} async-done(((bf16[8,2,128,128]{3,2,1,0:T(8,128)(2,1)}), bf16[8,2,128,128]{3,2,1,0:T(8,128)(2,1)S(1)}, u32[]{:S(2)}, u32[]{:S(2)}) %all-to-all-start.1) | async-done | bytes 524320 | tf_op jit(solution)/shard_map/all_to_all | solution.py:729
  101.7 1.4 %deliver.1 = f32[8,4,128,128]{3,2,1,0:T(8,128)} custom-call(bf16[8,2,128,128]{3,2,1,0:T(8,128)(2,1)S(1)} %all-to-all-done.refs_0_, bf16[8,2,128,128]{3,2,1,0:T(8,128)(2,1)S(1)} %all-to-all-done.1.refs_1_), custom_call_target="tpu_custom_call" | custom-call | tf_op jit(solution)/shard_map/deliver/pallas_call | solution.py:661
  (3 shorter events, 0.0 us)
Async XLA Ops:
  2.2 3.2 %collective-permute-start = (bf16[4,32,128]{2,1,0:T(8,128)(2,1)S(1)}, bf16[4,32,128]{2,1,0:T(8,128)(2,1)S(1)}, u32[]{:S(2)}, u32[]{:S(2)}) collective-permute-start(bf16[4,32,128]{2,1,0:T(8,128)(2,1)S(1)} %pad_maximum_fusion), channel_id=1, source_target_pairs={{0,8},{8,16},{16,24},{1,9},{9,17},{17,25},{2,10},{10,18},{18,26},{... | collective-permute-start | bytes 98312 | tf_op jit(solution)/shard_map/ppermute | solution.py:713
  30.2 27.5 %collective-permute-start.4 = (bf16[8,256,128]{2,1,0:T(8,128)(2,1)S(1)}, bf16[8,256,128]{2,1,0:T(8,128)(2,1)S(1)}, u32[]{:S(2)}, u32[]{:S(2)}) collective-permute-start(bf16[8,256,128]{2,1,0:T(8,128)(2,1)S(1)} %get-tuple-element.26.refs_1_), channel_id=1, source_target_pairs={{0,24},{8,16},{16,8},{24,0},{1,25},{9,17},{17,9},{25,1},{2,26},{10... | collective-permute-start | bytes 1572872 | tf_op jit(solution)/shard_map/ppermute | solution.py:674
  30.3 27.4 %collective-permute-start.3 = (bf16[8,256,128]{2,1,0:T(8,128)(2,1)S(1)}, bf16[8,256,128]{2,1,0:T(8,128)(2,1)S(1)}, u32[]{:S(2)}, u32[]{:S(2)}) collective-permute-start(bf16[8,256,128]{2,1,0:T(8,128)(2,1)S(1)} %get-tuple-element.26.refs_1_), channel_id=1, source_target_pairs={{0,16},{8,24},{16,0},{24,8},{1,17},{9,25},{17,1},{25,9},{2,18},{10... | collective-permute-start | bytes 1572872 | tf_op jit(solution)/shard_map/ppermute | solution.py:674
  34.7 23.1 %collective-permute-start.2 = (bf16[8,256,128]{2,1,0:T(8,128)(2,1)S(1)}, bf16[8,256,128]{2,1,0:T(8,128)(2,1)S(1)}, u32[]{:S(2)}, u32[]{:S(2)}) collective-permute-start(bf16[8,256,128]{2,1,0:T(8,128)(2,1)S(1)} %get-tuple-element.26.refs_1_), channel_id=1, source_target_pairs={{0,8},{8,0},{16,24},{24,16},{1,9},{9,1},{17,25},{25,17},{2,10},{10... | collective-permute-start | bytes 1572872 | tf_op jit(solution)/shard_map/ppermute | solution.py:674
  34.7 23.1 %copy-start = (s32[1,8]{1,0:T(1,128)S(1)}, s32[1,8]{1,0:T(1,128)}, u32[]{:S(2)}) copy-start(s32[1,8]{1,0:T(1,128)} %refs_0_.9) | copy-start | bytes 100
  57.2 8.5 %collective-permute-start.1 = (bf16[8,256,128]{2,1,0:T(8,128)(2,1)S(1)}, bf16[8,256,128]{2,1,0:T(8,128)(2,1)S(1)}, u32[]{:S(2)}, u32[]{:S(2)}) collective-permute-start(bf16[8,256,128]{2,1,0:T(8,128)(2,1)S(1)} %get-tuple-element.25.refs_1_), channel_id=1, source_target_pairs={{0,8},{8,0},{16,24},{24,16},{1,9},{9,1},{17,25},{25,17},{2,10},{10... | collective-permute-start | bytes 1572872 | tf_op jit(solution)/shard_map/ppermute | solution.py:674
  59.9 22.9 %all-to-all-start = ((bf16[8,2,128,128]{3,2,1,0:T(8,128)(2,1)}), bf16[8,2,128,128]{3,2,1,0:T(8,128)(2,1)S(1)}, u32[]{:S(2)}, u32[]{:S(2)}) async-start(bf16[8,2,128,128]{3,2,1,0:T(8,128)(2,1)} %get-tuple-element.36), calls=%async_computation | async-start | bytes 1048576 | tf_op jit(solution)/shard_map/all_to_all | solution.py:729
  67.1 13.6 %collective-permute-start.5 = (bf16[8,256,128]{2,1,0:T(8,128)(2,1)S(1)}, bf16[8,256,128]{2,1,0:T(8,128)(2,1)S(1)}, u32[]{:S(2)}, u32[]{:S(2)}) collective-permute-start(bf16[8,256,128]{2,1,0:T(8,128)(2,1)S(1)} %get-tuple-element.29.refs_3_), channel_id=1, source_target_pairs={{0,16},{8,24},{16,0},{24,8},{1,17},{9,25},{17,1},{25,9},{2,18},{10... | collective-permute-start | bytes 1572872 | tf_op jit(solution)/shard_map/ppermute | solution.py:681
  82.8 18.9 %all-to-all-start.1 = ((bf16[8,2,128,128]{3,2,1,0:T(8,128)(2,1)}), bf16[8,2,128,128]{3,2,1,0:T(8,128)(2,1)S(1)}, u32[]{:S(2)}, u32[]{:S(2)}) async-start(bf16[8,2,128,128]{3,2,1,0:T(8,128)(2,1)} %get-tuple-element.37), calls=%async_computation.1 | async-start | bytes 1048576 | tf_op jit(solution)/shard_map/all_to_all | solution.py:729

commit v5 on v4

--- a/solution.py
+++ b/solution.py
@@ -522,6 +522,37 @@
     )
 
 
+def last_rows(qk_rows, v_in, rim):
+    prompts, _, width = v_in.shape
+    tall = 2 * EDGE
+    heads = width // DV
+
+    def kernel(qk_ref, v_ref, out_ref):
+        for p in range(prompts):
+            out_ref[p, :tall] = qk_ref[p]
+            values = v_ref[p].astype(F32)
+            rows = [
+                values[tall - rim + i : tall - rim + i + 1, h * DV : (h + 1) * DV]
+                for i in range(rim)
+                for h in range(heads)
+            ]
+            rows.append(jnp.zeros((tall - rim * heads, DV), F32))
+            out_ref[p, tall:] = jnp.concatenate(rows, axis=0).astype(BF16)
+
+    return pl.pallas_call(
+        kernel,
+        grid=(1,),
+        in_specs=[
+            pl.BlockSpec((prompts, tall, DK), lambda i: (0, qk_rows.shape[1] // tall - 1, 0)),
+            pl.BlockSpec((prompts, tall, width), lambda i: (0, v_in.shape[1] // tall - 1, 0)),
+        ],
+        out_specs=pl.BlockSpec((prompts, 2 * tall, DK), lambda i: (0, 0, 0)),
+        out_shape=jax.ShapeDtypeStruct((prompts, 2 * tall, DK), BF16),
+        compiler_params=pltpu.CompilerParams(vmem_limit_bytes=SMALL_VMEM_BYTES),
+        name="last_rows",
+    )(far(qk_rows), far(v_in))
+
+
 def own_chip():
     seq = lax.axis_index("seq")
     return seq // 2, seq % 2 == 1
@@ -572,6 +603,7 @@
 
 
 def chain_maps(ins, outs):
+    ins = (ins[0],) + tuple(ins[:0:-1])
     count = len(ins)
     mine = lax.axis_index("seq")
     every = range(ins[0].shape[0])
@@ -697,19 +729,7 @@
 
     qk_rows = by_head(qk_in)
     qk_taps = by_head(conv_qk[None])[0]
-    qk_tail = qk_rows[:, (tok - rim) * 2 * key_heads :]
-    v_tail = v_in[:, tok - rim :].reshape(prompts, rim * value_heads, DV)
-    front = 2 * EDGE - qk_tail.shape[1]
-    back = 2 * EDGE - v_tail.shape[1]
-    tails = jnp.concatenate(
-        [
-            jnp.zeros((prompts, front, DK), BF16),
-            qk_tail,
-            v_tail,
-            jnp.zeros((prompts, back, DK), BF16),
-        ],
-        axis=1,
-    )
+    tails = last_rows(qk_rows, v_in, rim)
     halo = lax.ppermute(tails, "seq", [(i, i + 1) for i in range(seq_count - 1)])
     group = value_heads // key_heads
     chips = seq_count // 2
@@ -750,7 +770,7 @@
         if job == jobs[-1]:
             moved.append(across(own_map, 1))
         else:
-            moved += [across(own_map, k) for k in range(1, seq_count)]
+            moved += [across(own_map, k) for k in range(seq_count - 1, 0, -1)]
         made.append((*(mixed or new), wu, starts, moved))
 
     entered = []

time: 104 us -> 103 us (level)
  local copies, waits for them, and re-layouts: 1.53 us -> 0.01 us
    slice x2 -> x0, local copies, waits for them, and re-layouts: 1.5 us -> none  [the longest x1 0.77 us: shards(): v_tail = v_in[:, tok - rim:].reshape(prompts, rim * value_heads, DV)]
where the time goes in v5:
time: 103 us
  Pallas kernels  78.8 us (77%)
  starting transfers between devices  19 us (18%)
  waiting for transfers between devices  4.44 us (4%)
    pallas_call x2, Pallas kernels, prepare(): pl.pallas_call(functools.partial(prepare_kernel, first, count, head, grou...  47.4 us
    pallas_call x2, Pallas kernels, outputs(): pl.pallas_call(functools.partial(outputs_kernel, begin, head, group, chun...  23.5 us
    all_to_all x2, starting transfers between devices, finish(): sent[head] = lax.all_to_all(results[2], 'head', 0, 0)  11.6 us
    pallas_call x3, Pallas kernels, state_step(): pl.pallas_call(kernel, in_specs=[pl.BlockSpec(memory_space=pltpu.SMEM)] +...  5.61 us
    ppermute x4, starting transfers between devices, across(): return lax.ppermute(block, 'seq', [(i, i ^ distance) for i in range(count)])  4.91 us
    ppermute x1, starting transfers between devices, shards(): lax.ppermute(tails, 'seq', [(i, i + 1) for i in range(seq_count - 1)])  2.36 us
  transfers between devices with their start and end apart: 8, of which 3 were waited for; matrix products, arithmetic and copies ran while one was open for 0% of the time, Pallas kernels for 50%

profile of v5, /device:TPU:0, one launch (start us, length us, event | category | flops | bytes accessed | tf_op | source)
XLA Modules:
  0.0 102.9 jit_solution(2717381405064267537)
XLA Ops:
  0.6 0.9 last_rows.1
  1.5 2.4 %collective-permute-start = (bf16[4,32,128]{2,1,0:T(8,128)(2,1)S(1)}, bf16[4,32,128]{2,1,0:T(8,128)(2,1)S(1)}, u32[]{:S(2)}, u32[]{:S(2)}) collective-permute-start(bf16[4,32,128]{2,1,0:T(8,128)(2,1)S(1)} %last_rows.1), channel_id=1, source_target_pairs={{0,8},{8,16},{16,24},{1,9},{9,17},{17,25},{2,10},{10,18},{18,26},{... | collective-permute-start | bytes 98312 | tf_op jit(solution)/shard_map/ppermute | solution.py:733
  3.9 0.8 collective-permute-done.refs_2_
  4.7 24.9 %prepare.2 = (bf16[4,16,256,128]{3,2,1,0:T(8,128)(2,1)}, bf16[4,2,2048,128]{3,2,1,0:T(8,128)(2,1)}, bf16[8,256,128]{2,1,0:T(8,128)(2,1)S(1)}, f32[8,128]{1,0:T(8...) custom-call(s32[4]{0:T(128)} %length_ref.3, bf16[4,1024,512]{2,1,0:T(8,128)(2,1)} %refs_1_.3, ...), custom_call_target="tpu_custom_call" | custom-call | flops 20000000000 | bytes 16777216 | tf_op jit(solution)/shard_map/prepare/pallas_call | solution.py:394
  29.6 2.8 %collective-permute-start.4 = (bf16[8,256,128]{2,1,0:T(8,128)(2,1)S(1)}, bf16[8,256,128]{2,1,0:T(8,128)(2,1)S(1)}, u32[]{:S(2)}, u32[]{:S(2)}) collective-permute-start(bf16[8,256,128]{2,1,0:T(8,128)(2,1)S(1)} %get-tuple-element.26.refs_1_), channel_id=1, source_target_pairs={{0,8},{8,0},{16,24},{24,16},{1,9},{9,1},{17,25},{25,17},{2,10},{10... | collective-permute-start | bytes 1572872 | tf_op jit(solution)/shard_map/ppermute | solution.py:706
  32.3 0.0 collective-permute-start.3
  32.4 1.4 %collective-permute-start.2 = (bf16[8,256,128]{2,1,0:T(8,128)(2,1)S(1)}, bf16[8,256,128]{2,1,0:T(8,128)(2,1)S(1)}, u32[]{:S(2)}, u32[]{:S(2)}) collective-permute-start(bf16[8,256,128]{2,1,0:T(8,128)(2,1)S(1)} %get-tuple-element.26.refs_1_), channel_id=1, source_target_pairs={{0,24},{8,16},{16,8},{24,0},{1,25},{9,17},{17,9},{25,1},{2,26},{10... | collective-permute-start | bytes 1572872 | tf_op jit(solution)/shard_map/ppermute | solution.py:706
  33.8 0.0 copy-start
  33.8 22.5 %prepare.3 = (bf16[4,16,256,128]{3,2,1,0:T(8,128)(2,1)}, bf16[4,2,2048,128]{3,2,1,0:T(8,128)(2,1)}, bf16[8,256,128]{2,1,0:T(8,128)(2,1)S(1)}, f32[8,128]{1,0:T(8,128)}) custom-call(s32[4]{0:T(128)} %length_ref.3, bf16[4,1024,512]{2,1,0:T(8,128)(2,1)} %refs_1_.3, bf16[4,32,128]{2,1,0:T(8,128)(2,1)S(1)} %collective-permute-done.refs_2_, ...), custom_call_target="tpu_custom_call" | custom-call | flops 20000000000 | bytes 16777216 | tf_op jit(solution)/shard_map/prepare/pallas_call | solution.py:394
  56.3 0.7 collective-permute-start.1
  57.0 0.0 collective-permute-done.4.refs_4_
  57.0 0.0 collective-permute-done.3.refs_3_
  57.0 0.0 collective-permute-done.2.refs_2_
  57.0 0.0 copy-done
  57.1 2.2 %state_step.3 = (bf16[8,128,128]{2,1,0:T(8,128)(2,1)S(1)}, bf16[8,128,128]{2,1,0:T(8,128)(2,1)}, bf16[8,2,128,128]{3,2,1,0:T(8,128)(2,1)}, f32[8,128]{1,0:T(8,128)}) custom-call(s32[1,8]{1,0:T(1,128)S(1)} %copy-done, bf16[8,256,128]{2,1,0:T(8,128)(2,1)S(1)} %get-tuple-element.26.refs_1_, bf16[8,256,128]{2,1,0:T(8,128)(2,1)S(1)} %collective-permute-done.2.refs_2_, ...), custom_call_target="tpu_custom_call" | custom-call | flops 1000000000 | bytes 1048576 | tf_op jit(solution)/shard_map/state_step/pallas_call | solution.py:673
  59.2 5.8 %all-to-all-start = ((bf16[8,2,128,128]{3,2,1,0:T(8,128)(2,1)}), bf16[8,2,128,128]{3,2,1,0:T(8,128)(2,1)S(1)}, u32[]{:S(2)}, u32[]{:S(2)}) async-start(bf16[8,2,128,128]{3,2,1,0:T(8,128)(2,1)} %get-tuple-element.36), calls=%async_computation | async-start | bytes 1048576 | tf_op jit(solution)/shard_map/all_to_all | solution.py:749
  65.1 0.0 collective-permute-done.1.refs_2_
  65.1 1.4 %state_step.4 = (bf16[8,256,128]{2,1,0:T(8,128)(2,1)S(1)}, f32[8,128]{1,0:T(8,128)}) custom-call(s32[1,8]{1,0:T(1,128)S(1)} %copy-done, bf16[8,256,128]{2,1,0:T(8,128)(2,1)S(1)} %get-tuple-element.25.refs_1_, bf16[8,256,128]{2,1,0:T(8,128)(2,1)S(1)} %collective-permute-done.1.refs_2_, f32[8,128]{1,0:T(8,128)} %get-tuple-element.28.refs_3_), custom_call_target="tpu_custom_call" | custom-call | flops 1000000000 | bytes 1048576 | tf_op jit(solution)/shard_map/state_step/pallas_call | solution.py:673
  66.4 0.2 collective-permute-start.5
  66.6 11.9 %outputs.2.refs_5_.held_ref = bf16[4,1024,512]{2,1,0:T(8,128)(2,1)} custom-call(s32[4]{0:T(128)} %length_ref.3, bf16[4,1024,256]{2,1,0:T(8,128)(2,1)} %get-tuple-element.20.qn_ref, bf16[4,1024,256]{2,1,0:T(8,128)(2,1)} %get-tuple-element.21.refs_7_.kn_ref, bf16[4,16,256,128]{3,2,1,0:T(8,128)(2,1)} %get-tuple-element.30.wu_ref, ...), custom_call_target="tpu_custom_call" | custom-call | flops 12000000000 | bytes 16777216 | tf_op jit(solution)/shard_map/outputs/pallas_call | solution.py:489
  78.6 1.7 %collective-permute-done.5.refs_4_ = bf16[8,256,128]{2,1,0:T(8,128)(2,1)S(1)} collective-permute-done((bf16[8,256,128]{2,1,0:T(8,128)(2,1)S(1)}, bf16[8,256,128]{2,1,0:T(8,128)(2,1)S(1)}, u32[]{:S(2)}, u32[]{:S(2)}) %collective-permute-start.5) | collective-permute-done | bytes 524320 | tf_op jit(solution)/shard_map/ppermute | solution.py:713
  80.2 2.1 %state_step.5 = (bf16[8,128,128]{2,1,0:T(8,128)(2,1)S(1)}, bf16[8,128,128]{2,1,0:T(8,128)(2,1)}, bf16[8,2,128,128]{3,2,1,0:T(8,128)(2,1)}, f32[8,128]{1,0:T(8,128)}) custom-call(s32[1,8]{1,0:T(1,128)S(1)} %copy-done, bf16[8,256,128]{2,1,0:T(8,128)(2,1)S(1)} %get-tuple-element.25.refs_1_, bf16[8,256,128]{2,1,0:T(8,128)(2,1)S(1)} %collective-permute-done.1.refs_2_, ...), custom_call_target="tpu_custom_call" | custom-call | flops 1000000000 | bytes 1048576 | tf_op jit(solution)/shard_map/state_step/pallas_call | solution.py:673
  82.3 0.0 all-to-all-done.refs_0_
  82.3 5.7 %all-to-all-start.1 = ((bf16[8,2,128,128]{3,2,1,0:T(8,128)(2,1)}), bf16[8,2,128,128]{3,2,1,0:T(8,128)(2,1)S(1)}, u32[]{:S(2)}, u32[]{:S(2)}) async-start(bf16[8,2,128,128]{3,2,1,0:T(8,128)(2,1)} %get-tuple-element.37), calls=%async_computation.1 | async-start | bytes 1048576 | tf_op jit(solution)/shard_map/all_to_all | solution.py:749
  88.0 11.6 %outputs.3 = bf16[4,1024,512]{2,1,0:T(8,128)(2,1)} custom-call(s32[4]{0:T(128)} %length_ref.3, bf16[4,1024,256]{2,1,0:T(8,128)(2,1)} %get-tuple-element.20.qn_ref, bf16[4,1024,256]{2,1,0:T(8,128)(2,1)} %get-tuple-element.21.refs_7_.kn_ref, bf16[4,16,256,128]{3,2,1,0:T(8,128)(2,1)} %get-tuple-element.23.wu_ref, ...), custom_call_target="tpu_custom_call", output_to_operand_aliasing={{}: (10, {})} | custom-call | flops 12000000000 | bytes 16777216 | tf_op jit(solution)/shard_map/outputs/pallas_call | solution.py:489
  99.6 1.9 %all-to-all-done.1.refs_1_ = bf16[8,2,128,128]{3,2,1,0:T(8,128)(2,1)S(1)} async-done(((bf16[8,2,128,128]{3,2,1,0:T(8,128)(2,1)}), bf16[8,2,128,128]{3,2,1,0:T(8,128)(2,1)S(1)}, u32[]{:S(2)}, u32[]{:S(2)}) %all-to-all-start.1) | async-done | bytes 524320 | tf_op jit(solution)/shard_map/all_to_all | solution.py:749
  101.5 1.4 %deliver.1 = f32[8,4,128,128]{3,2,1,0:T(8,128)} custom-call(bf16[8,2,128,128]{3,2,1,0:T(8,128)(2,1)S(1)} %all-to-all-done.refs_0_, bf16[8,2,128,128]{3,2,1,0:T(8,128)(2,1)S(1)} %all-to-all-done.1.refs_1_), custom_call_target="tpu_custom_call" | custom-call | tf_op jit(solution)/shard_map/deliver/pallas_call | solution.py:693
Async XLA Ops:
  1.5 3.2 %collective-permute-start = (bf16[4,32,128]{2,1,0:T(8,128)(2,1)S(1)}, bf16[4,32,128]{2,1,0:T(8,128)(2,1)S(1)}, u32[]{:S(2)}, u32[]{:S(2)}) collective-permute-start(bf16[4,32,128]{2,1,0:T(8,128)(2,1)S(1)} %last_rows.1), channel_id=1, source_target_pairs={{0,8},{8,16},{16,24},{1,9},{9,17},{17,25},{2,10},{10,18},{18,26},{... | collective-permute-start | bytes 98312 | tf_op jit(solution)/shard_map/ppermute | solution.py:733
  29.6 27.5 %collective-permute-start.4 = (bf16[8,256,128]{2,1,0:T(8,128)(2,1)S(1)}, bf16[8,256,128]{2,1,0:T(8,128)(2,1)S(1)}, u32[]{:S(2)}, u32[]{:S(2)}) collective-permute-start(bf16[8,256,128]{2,1,0:T(8,128)(2,1)S(1)} %get-tuple-element.26.refs_1_), channel_id=1, source_target_pairs={{0,8},{8,0},{16,24},{24,16},{1,9},{9,1},{17,25},{25,17},{2,10},{10... | collective-permute-start | bytes 1572872 | tf_op jit(solution)/shard_map/ppermute | solution.py:706
  32.3 24.7 %collective-permute-start.3 = (bf16[8,256,128]{2,1,0:T(8,128)(2,1)S(1)}, bf16[8,256,128]{2,1,0:T(8,128)(2,1)S(1)}, u32[]{:S(2)}, u32[]{:S(2)}) collective-permute-start(bf16[8,256,128]{2,1,0:T(8,128)(2,1)S(1)} %get-tuple-element.26.refs_1_), channel_id=1, source_target_pairs={{0,16},{8,24},{16,0},{24,8},{1,17},{9,25},{17,1},{25,9},{2,18},{10... | collective-permute-start | bytes 1572872 | tf_op jit(solution)/shard_map/ppermute | solution.py:706
  32.4 24.7 %collective-permute-start.2 = (bf16[8,256,128]{2,1,0:T(8,128)(2,1)S(1)}, bf16[8,256,128]{2,1,0:T(8,128)(2,1)S(1)}, u32[]{:S(2)}, u32[]{:S(2)}) collective-permute-start(bf16[8,256,128]{2,1,0:T(8,128)(2,1)S(1)} %get-tuple-element.26.refs_1_), channel_id=1, source_target_pairs={{0,24},{8,16},{16,8},{24,0},{1,25},{9,17},{17,9},{25,1},{2,26},{10... | collective-permute-start | bytes 1572872 | tf_op jit(solution)/shard_map/ppermute | solution.py:706
  33.8 23.3 %copy-start = (s32[1,8]{1,0:T(1,128)S(1)}, s32[1,8]{1,0:T(1,128)}, u32[]{:S(2)}) copy-start(s32[1,8]{1,0:T(1,128)} %refs_0_.9) | copy-start | bytes 100
  56.3 8.7 %collective-permute-start.1 = (bf16[8,256,128]{2,1,0:T(8,128)(2,1)S(1)}, bf16[8,256,128]{2,1,0:T(8,128)(2,1)S(1)}, u32[]{:S(2)}, u32[]{:S(2)}) collective-permute-start(bf16[8,256,128]{2,1,0:T(8,128)(2,1)S(1)} %get-tuple-element.25.refs_1_), channel_id=1, source_target_pairs={{0,8},{8,0},{16,24},{24,16},{1,9},{9,1},{17,25},{25,17},{2,10},{10... | collective-permute-start | bytes 1572872 | tf_op jit(solution)/shard_map/ppermute | solution.py:706
  59.2 23.1 %all-to-all-start = ((bf16[8,2,128,128]{3,2,1,0:T(8,128)(2,1)}), bf16[8,2,128,128]{3,2,1,0:T(8,128)(2,1)S(1)}, u32[]{:S(2)}, u32[]{:S(2)}) async-start(bf16[8,2,128,128]{3,2,1,0:T(8,128)(2,1)} %get-tuple-element.36), calls=%async_computation | async-start | bytes 1048576 | tf_op jit(solution)/shard_map/all_to_all | solution.py:749
  66.4 13.8 %collective-permute-start.5 = (bf16[8,256,128]{2,1,0:T(8,128)(2,1)S(1)}, bf16[8,256,128]{2,1,0:T(8,128)(2,1)S(1)}, u32[]{:S(2)}, u32[]{:S(2)}) collective-permute-start(bf16[8,256,128]{2,1,0:T(8,128)(2,1)S(1)} %get-tuple-element.29.refs_3_), channel_id=1, source_target_pairs={{0,16},{8,24},{16,0},{24,8},{1,17},{9,25},{17,1},{25,9},{2,18},{10... | collective-permute-start | bytes 1572872 | tf_op jit(solution)/shard_map/ppermute | solution.py:713
  82.3 19.2 %all-to-all-start.1 = ((bf16[8,2,128,128]{3,2,1,0:T(8,128)(2,1)}), bf16[8,2,128,128]{3,2,1,0:T(8,128)(2,1)S(1)}, u32[]{:S(2)}, u32[]{:S(2)}) async-start(bf16[8,2,128,128]{3,2,1,0:T(8,128)(2,1)} %get-tuple-element.37), calls=%async_computation.1 | async-start | bytes 1048576 | tf_op jit(solution)/shard_map/all_to_all | solution.py:749

commit v6 on v5

--- a/solution.py
+++ b/solution.py
@@ -109,7 +109,7 @@
     rim = 2 * EDGE
     taps = taps_ref[...].astype(F32)
     raw_scr[:rim] = halo_ref[0].astype(F32)[:rim]
-    raw_scr[rim:] = qk_ref[0].astype(F32)
+    raw_scr[rim : rim + qk_ref.shape[1]] = qk_ref[0].astype(F32)
     for c in range(chunks):
         span = slice(c * BLOCK, (c + 1) * BLOCK)
         for kind in range(kinds):
@@ -370,7 +370,7 @@
         pltpu.HBM((8, 128), F32),
     ]
     scratch = [
-        pltpu.VMEM((tok * group + EDGE, DV), F32),
+        pltpu.VMEM((tok * group + 2 * EDGE, DV), F32),
         pltpu.VMEM((2, chunks, group, DK, DK), BF16),
         pltpu.VMEM((2, chunks, group, DV, DK), F32),
         pltpu.VMEM((2, chunks, group, BLOCK), F32),
@@ -387,7 +387,7 @@
         ]
         out_specs += [pl.BlockSpec((1, tok, key_heads * DK), lambda i, lengths: (now(i), 0, 0))] * 2
         out_shape += [pltpu.HBM((count, tok, key_heads * DK), BF16)] * 2
-        scratch.append(pltpu.VMEM((qk_rows.shape[1] + 2 * EDGE, DK), F32))
+        scratch.append(pltpu.VMEM((qk_rows.shape[1] + 3 * EDGE, DK), F32))
     else:
         operands.append(far(mixed))
         in_specs.append(pl.BlockSpec((1, tok, DK), lambda i, lengths: (first + now(i), 0, head)))

time: 103 us -> 103 us (level); the launches traced: 103 us -> 101 us
  starting transfers between devices: 19 us -> 17.1 us
    ppermute x4, starting transfers between devices: 4.91 us -> 1.88 us  [across(): return lax.ppermute(block, 'seq', [(i, i ^ distance) for i in range(count)])]
  transfers between devices with their start and end apart: 8 -> 8, of which waited for: 3 -> 4; matrix products, arithmetic and copies ran while one was open for 0% -> 0% of each run, Pallas kernels for 50% -> 51%
where the time goes in v6:
time: 103 us; the launch traced here: 101 us
  Pallas kernels  78.9 us (77%)
  starting transfers between devices  17.1 us (17%)
  waiting for transfers between devices  4.83 us (5%)
    pallas_call x2, Pallas kernels, prepare(): pl.pallas_call(functools.partial(prepare_kernel, first, count, head, grou...  47.5 us
    pallas_call x2, Pallas kernels, outputs(): pl.pallas_call(functools.partial(outputs_kernel, begin, head, group, chun...  23.5 us
    all_to_all x2, starting transfers between devices, finish(): sent[head] = lax.all_to_all(results[2], 'head', 0, 0)  12.4 us
    pallas_call x3, Pallas kernels, state_step(): pl.pallas_call(kernel, in_specs=[pl.BlockSpec(memory_space=pltpu.SMEM)] +...  5.61 us
    ppermute x1, starting transfers between devices, shards(): lax.ppermute(tails, 'seq', [(i, i + 1) for i in range(seq_count - 1)])  2.36 us
  transfers between devices with their start and end apart: 8, of which 4 were waited for; matrix products, arithmetic and copies ran while one was open for 0% of the time, Pallas kernels for 51%

profile of v6, /device:TPU:0, one launch (start us, length us, event | category | flops | bytes accessed | tf_op | source)
XLA Modules:
  0.0 101.5 jit_solution(15816669839652792511)
XLA Ops:
  0.6 0.9 last_rows.1
  1.5 2.4 %collective-permute-start = (bf16[4,32,128]{2,1,0:T(8,128)(2,1)S(1)}, bf16[4,32,128]{2,1,0:T(8,128)(2,1)S(1)}, u32[]{:S(2)}, u32[]{:S(2)}) collective-permute-start(bf16[4,32,128]{2,1,0:T(8,128)(2,1)S(1)} %last_rows.1), channel_id=1, source_target_pairs={{0,8},{8,16},{16,24},{1,9},{9,17},{17,25},{2,10},{10,18},{18,26},{... | collective-permute-start | bytes 98312 | tf_op jit(solution)/shard_map/ppermute | solution.py:733
  3.9 0.8 collective-permute-done.refs_2_
  4.7 24.9 %prepare.2 = (bf16[4,16,256,128]{3,2,1,0:T(8,128)(2,1)}, bf16[4,2,2048,128]{3,2,1,0:T(8,128)(2,1)}, bf16[8,256,128]{2,1,0:T(8,128)(2,1)S(1)}, f32[8,128]{1,0:T(8...) custom-call(s32[4]{0:T(128)} %length_ref.3, bf16[4,1024,512]{2,1,0:T(8,128)(2,1)} %refs_1_.3, ...), custom_call_target="tpu_custom_call" | custom-call | flops 20000000000 | bytes 16777216 | tf_op jit(solution)/shard_map/prepare/pallas_call | solution.py:394
  29.6 0.0 collective-permute-start.4
  29.7 0.1 collective-permute-start.3
  29.8 1.8 %collective-permute-start.2 = (bf16[8,256,128]{2,1,0:T(8,128)(2,1)S(1)}, bf16[8,256,128]{2,1,0:T(8,128)(2,1)S(1)}, u32[]{:S(2)}, u32[]{:S(2)}) collective-permute-start(bf16[8,256,128]{2,1,0:T(8,128)(2,1)S(1)} %get-tuple-element.26.refs_1_), channel_id=1, source_target_pairs={{0,24},{8,16},{16,8},{24,0},{1,25},{9,17},{17,9},{25,1},{2,26},{10... | collective-permute-start | bytes 1572872 | tf_op jit(solution)/shard_map/ppermute | solution.py:706
  31.5 0.0 copy-start
  31.5 22.6 %prepare.3 = (bf16[4,16,256,128]{3,2,1,0:T(8,128)(2,1)}, bf16[4,2,2048,128]{3,2,1,0:T(8,128)(2,1)}, bf16[8,256,128]{2,1,0:T(8,128)(2,1)S(1)}, f32[8,128]{1,0:T(8,128)}) custom-call(s32[4]{0:T(128)} %length_ref.3, bf16[4,1024,512]{2,1,0:T(8,128)(2,1)} %refs_1_.3, bf16[4,32,128]{2,1,0:T(8,128)(2,1)S(1)} %collective-permute-done.refs_2_, ...), custom_call_target="tpu_custom_call" | custom-call | flops 20000000000 | bytes 16777216 | tf_op jit(solution)/shard_map/prepare/pallas_call | solution.py:394
  54.1 0.0 collective-permute-start.1
  54.1 0.0 collective-permute-done.4.refs_4_
  54.1 0.0 collective-permute-done.3.refs_3_
  54.2 0.6 collective-permute-done.2.refs_2_
  54.8 0.0 copy-done
  54.8 2.1 %state_step.3 = (bf16[8,128,128]{2,1,0:T(8,128)(2,1)S(1)}, bf16[8,128,128]{2,1,0:T(8,128)(2,1)}, bf16[8,2,128,128]{3,2,1,0:T(8,128)(2,1)}, f32[8,128]{1,0:T(8,128)}) custom-call(s32[1,8]{1,0:T(1,128)S(1)} %copy-done, bf16[8,256,128]{2,1,0:T(8,128)(2,1)S(1)} %get-tuple-element.26.refs_1_, bf16[8,256,128]{2,1,0:T(8,128)(2,1)S(1)} %collective-permute-done.2.refs_2_, ...), custom_call_target="tpu_custom_call" | custom-call | flops 1000000000 | bytes 1048576 | tf_op jit(solution)/shard_map/state_step/pallas_call | solution.py:673
  56.9 6.7 %all-to-all-start = ((bf16[8,2,128,128]{3,2,1,0:T(8,128)(2,1)}), bf16[8,2,128,128]{3,2,1,0:T(8,128)(2,1)S(1)}, u32[]{:S(2)}, u32[]{:S(2)}) async-start(bf16[8,2,128,128]{3,2,1,0:T(8,128)(2,1)} %get-tuple-element.36), calls=%async_computation | async-start | bytes 1048576 | tf_op jit(solution)/shard_map/all_to_all | solution.py:749
  63.6 0.0 collective-permute-done.1.refs_2_
  63.6 1.4 %state_step.4 = (bf16[8,256,128]{2,1,0:T(8,128)(2,1)S(1)}, f32[8,128]{1,0:T(8,128)}) custom-call(s32[1,8]{1,0:T(1,128)S(1)} %copy-done, bf16[8,256,128]{2,1,0:T(8,128)(2,1)S(1)} %get-tuple-element.25.refs_1_, bf16[8,256,128]{2,1,0:T(8,128)(2,1)S(1)} %collective-permute-done.1.refs_2_, f32[8,128]{1,0:T(8,128)} %get-tuple-element.28.refs_3_), custom_call_target="tpu_custom_call" | custom-call | flops 1000000000 | bytes 1048576 | tf_op jit(solution)/shard_map/state_step/pallas_call | solution.py:673
  65.0 0.5 collective-permute-start.5
  65.4 11.9 %outputs.2.refs_5_.held_ref = bf16[4,1024,512]{2,1,0:T(8,128)(2,1)} custom-call(s32[4]{0:T(128)} %length_ref.3, bf16[4,1024,256]{2,1,0:T(8,128)(2,1)} %get-tuple-element.20.qn_ref, bf16[4,1024,256]{2,1,0:T(8,128)(2,1)} %get-tuple-element.21.refs_7_.kn_ref, bf16[4,16,256,128]{3,2,1,0:T(8,128)(2,1)} %get-tuple-element.30.wu_ref, ...), custom_call_target="tpu_custom_call" | custom-call | flops 12000000000 | bytes 16777216 | tf_op jit(solution)/shard_map/outputs/pallas_call | solution.py:489
  77.4 1.4 %collective-permute-done.5.refs_4_ = bf16[8,256,128]{2,1,0:T(8,128)(2,1)S(1)} collective-permute-done((bf16[8,256,128]{2,1,0:T(8,128)(2,1)S(1)}, bf16[8,256,128]{2,1,0:T(8,128)(2,1)S(1)}, u32[]{:S(2)}, u32[]{:S(2)}) %collective-permute-start.5) | collective-permute-done | bytes 524320 | tf_op jit(solution)/shard_map/ppermute | solution.py:713
  78.8 2.1 %state_step.5 = (bf16[8,128,128]{2,1,0:T(8,128)(2,1)S(1)}, bf16[8,128,128]{2,1,0:T(8,128)(2,1)}, bf16[8,2,128,128]{3,2,1,0:T(8,128)(2,1)}, f32[8,128]{1,0:T(8,128)}) custom-call(s32[1,8]{1,0:T(1,128)S(1)} %copy-done, bf16[8,256,128]{2,1,0:T(8,128)(2,1)S(1)} %get-tuple-element.25.refs_1_, bf16[8,256,128]{2,1,0:T(8,128)(2,1)S(1)} %collective-permute-done.1.refs_2_, ...), custom_call_target="tpu_custom_call" | custom-call | flops 1000000000 | bytes 1048576 | tf_op jit(solution)/shard_map/state_step/pallas_call | solution.py:673
  80.9 0.0 all-to-all-done.refs_0_
  80.9 5.7 %all-to-all-start.1 = ((bf16[8,2,128,128]{3,2,1,0:T(8,128)(2,1)}), bf16[8,2,128,128]{3,2,1,0:T(8,128)(2,1)S(1)}, u32[]{:S(2)}, u32[]{:S(2)}) async-start(bf16[8,2,128,128]{3,2,1,0:T(8,128)(2,1)} %get-tuple-element.37), calls=%async_computation.1 | async-start | bytes 1048576 | tf_op jit(solution)/shard_map/all_to_all | solution.py:749
  86.6 11.6 %outputs.3 = bf16[4,1024,512]{2,1,0:T(8,128)(2,1)} custom-call(s32[4]{0:T(128)} %length_ref.3, bf16[4,1024,256]{2,1,0:T(8,128)(2,1)} %get-tuple-element.20.qn_ref, bf16[4,1024,256]{2,1,0:T(8,128)(2,1)} %get-tuple-element.21.refs_7_.kn_ref, bf16[4,16,256,128]{3,2,1,0:T(8,128)(2,1)} %get-tuple-element.23.wu_ref, ...), custom_call_target="tpu_custom_call", output_to_operand_aliasing={{}: (10, {})} | custom-call | flops 12000000000 | bytes 16777216 | tf_op jit(solution)/shard_map/outputs/pallas_call | solution.py:489
  98.2 1.9 %all-to-all-done.1.refs_1_ = bf16[8,2,128,128]{3,2,1,0:T(8,128)(2,1)S(1)} async-done(((bf16[8,2,128,128]{3,2,1,0:T(8,128)(2,1)}), bf16[8,2,128,128]{3,2,1,0:T(8,128)(2,1)S(1)}, u32[]{:S(2)}, u32[]{:S(2)}) %all-to-all-start.1) | async-done | bytes 524320 | tf_op jit(solution)/shard_map/all_to_all | solution.py:749
  100.1 1.4 %deliver.1 = f32[8,4,128,128]{3,2,1,0:T(8,128)} custom-call(bf16[8,2,128,128]{3,2,1,0:T(8,128)(2,1)S(1)} %all-to-all-done.refs_0_, bf16[8,2,128,128]{3,2,1,0:T(8,128)(2,1)S(1)} %all-to-all-done.1.refs_1_), custom_call_target="tpu_custom_call" | custom-call | tf_op jit(solution)/shard_map/deliver/pallas_call | solution.py:693
Async XLA Ops:
  1.5 3.2 %collective-permute-start = (bf16[4,32,128]{2,1,0:T(8,128)(2,1)S(1)}, bf16[4,32,128]{2,1,0:T(8,128)(2,1)S(1)}, u32[]{:S(2)}, u32[]{:S(2)}) collective-permute-start(bf16[4,32,128]{2,1,0:T(8,128)(2,1)S(1)} %last_rows.1), channel_id=1, source_target_pairs={{0,8},{8,16},{16,24},{1,9},{9,17},{17,25},{2,10},{10,18},{18,26},{... | collective-permute-start | bytes 98312 | tf_op jit(solution)/shard_map/ppermute | solution.py:733
  29.6 24.5 %collective-permute-start.4 = (bf16[8,256,128]{2,1,0:T(8,128)(2,1)S(1)}, bf16[8,256,128]{2,1,0:T(8,128)(2,1)S(1)}, u32[]{:S(2)}, u32[]{:S(2)}) collective-permute-start(bf16[8,256,128]{2,1,0:T(8,128)(2,1)S(1)} %get-tuple-element.26.refs_1_), channel_id=1, source_target_pairs={{0,8},{8,0},{16,24},{24,16},{1,9},{9,1},{17,25},{25,17},{2,10},{10... | collective-permute-start | bytes 1572872 | tf_op jit(solution)/shard_map/ppermute | solution.py:706
  29.7 24.5 %collective-permute-start.3 = (bf16[8,256,128]{2,1,0:T(8,128)(2,1)S(1)}, bf16[8,256,128]{2,1,0:T(8,128)(2,1)S(1)}, u32[]{:S(2)}, u32[]{:S(2)}) collective-permute-start(bf16[8,256,128]{2,1,0:T(8,128)(2,1)S(1)} %get-tuple-element.26.refs_1_), channel_id=1, source_target_pairs={{0,16},{8,24},{16,0},{24,8},{1,17},{9,25},{17,1},{25,9},{2,18},{10... | collective-permute-start | bytes 1572872 | tf_op jit(solution)/shard_map/ppermute | solution.py:706
  29.8 25.0 %collective-permute-start.2 = (bf16[8,256,128]{2,1,0:T(8,128)(2,1)S(1)}, bf16[8,256,128]{2,1,0:T(8,128)(2,1)S(1)}, u32[]{:S(2)}, u32[]{:S(2)}) collective-permute-start(bf16[8,256,128]{2,1,0:T(8,128)(2,1)S(1)} %get-tuple-element.26.refs_1_), channel_id=1, source_target_pairs={{0,24},{8,16},{16,8},{24,0},{1,25},{9,17},{17,9},{25,1},{2,26},{10... | collective-permute-start | bytes 1572872 | tf_op jit(solution)/shard_map/ppermute | solution.py:706
  31.5 23.3 %copy-start = (s32[1,8]{1,0:T(1,128)S(1)}, s32[1,8]{1,0:T(1,128)}, u32[]{:S(2)}) copy-start(s32[1,8]{1,0:T(1,128)} %refs_0_.9) | copy-start | bytes 100
  54.1 9.5 %collective-permute-start.1 = (bf16[8,256,128]{2,1,0:T(8,128)(2,1)S(1)}, bf16[8,256,128]{2,1,0:T(8,128)(2,1)S(1)}, u32[]{:S(2)}, u32[]{:S(2)}) collective-permute-start(bf16[8,256,128]{2,1,0:T(8,128)(2,1)S(1)} %get-tuple-element.25.refs_1_), channel_id=1, source_target_pairs={{0,8},{8,0},{16,24},{24,16},{1,9},{9,1},{17,25},{25,17},{2,10},{10... | collective-permute-start | bytes 1572872 | tf_op jit(solution)/shard_map/ppermute | solution.py:706
  56.9 24.0 %all-to-all-start = ((bf16[8,2,128,128]{3,2,1,0:T(8,128)(2,1)}), bf16[8,2,128,128]{3,2,1,0:T(8,128)(2,1)S(1)}, u32[]{:S(2)}, u32[]{:S(2)}) async-start(bf16[8,2,128,128]{3,2,1,0:T(8,128)(2,1)} %get-tuple-element.36), calls=%async_computation | async-start | bytes 1048576 | tf_op jit(solution)/shard_map/all_to_all | solution.py:749
  65.0 13.8 %collective-permute-start.5 = (bf16[8,256,128]{2,1,0:T(8,128)(2,1)S(1)}, bf16[8,256,128]{2,1,0:T(8,128)(2,1)S(1)}, u32[]{:S(2)}, u32[]{:S(2)}) collective-permute-start(bf16[8,256,128]{2,1,0:T(8,128)(2,1)S(1)} %get-tuple-element.29.refs_3_), channel_id=1, source_target_pairs={{0,16},{8,24},{16,0},{24,8},{1,17},{9,25},{17,1},{25,9},{2,18},{10... | collective-permute-start | bytes 1572872 | tf_op jit(solution)/shard_map/ppermute | solution.py:713
  80.9 19.2 %all-to-all-start.1 = ((bf16[8,2,128,128]{3,2,1,0:T(8,128)(2,1)}), bf16[8,2,128,128]{3,2,1,0:T(8,128)(2,1)S(1)}, u32[]{:S(2)}, u32[]{:S(2)}) async-start(bf16[8,2,128,128]{3,2,1,0:T(8,128)(2,1)} %get-tuple-element.37), calls=%async_computation.1 | async-start | bytes 1048576 | tf_op jit(solution)/shard_map/all_to_all | solution.py:749
